TPU v7x, 256 devices: a whole 4x4x8 slice. The times are simulated.
256 devices in a mesh: lat: 64 (over x, z, core), lev: 4 (over y).
Axes of the slice: x: 4, y: 4, z: 8, core: 2. Of those that a mesh axis runs over, the one named last changes fastest.
Arguments:
- tendency: float32 [16, 2048, 4096], P('lev', 'lat'), may hold values from -6 to 6
- spectral: float32 [256, 2, 16, 2049], P(('lat', 'lev')), may hold values from -6 to 6
- panel: float32 [256, 2049, 1024], P(('lat', 'lev')), may hold values from -0.1875 to 0.1875
- quad_weights: float32 [1024], replicated, may hold values from 0.3 to 3
- diffusion: float32 [16], replicated, may hold values from 0.05 to 20
- waves: int32 [256], replicated, may hold values from 0 to 1023, as said below
- bounds: int32 [16, 2], replicated, may hold values from -14 to 142, as said below
Outputs:
- remapped: float32 [16, 2048, 4096], P('lev', 'lat')
- spectral_new: float32 [256, 2, 16, 2049], P(('lat', 'lev'))
Inputs may be any that keep to these rules, and one draw needn't show every extreme that they name: `waves`: all values distinct. For every k, k * 8 - 2 * 8 + 2 <= bounds[k,0] <= k * 8 and (k + 1) * 8 <= bounds[k,1] <= (k + 1) * 8 + 2 * 8 - 2.
All inputs are finite; a program needn't handle non-finite values.
Results may differ from a plain program's by a relative error of at most 0.0003.
Values sent between devices are 32-bit elements; how exact they have to be, the bound alone decides.
No kernel may reach another device: no remote copies, remote signals or barrier semaphores. Data moves between devices by JAX's collectives and lax.ppermute only.
A program may use at most 64 MiB of HBM per device.

v0:
```python
import math

import jax
import jax.numpy as jnp
from jax import lax
from jax.experimental import pallas as pl
from jax.experimental.pallas import tpu as pltpu
from jax.sharding import PartitionSpec as P

NTRUNC = 2048
SUBDIV = 8
NLON = 4096
FOLD = NLON // 2
PAIRS = 256
ROWS = 2049
HALF = 1024
LEV = 16
PAIR_BLOCK = 64
ROW_BLOCK = 256
ROW_STEPS = -(-ROWS // ROW_BLOCK)
LON_BLOCK = 512
VMEM = 56 * 1024 * 1024
NT = (((1,), (1,)), ((), ()))
NN = (((1,), (0,)), ((), ()))


def split(value):
    high = value.astype(jnp.bfloat16)
    low = (value - high.astype(jnp.float32)).astype(jnp.bfloat16)
    return (high, low)


def mxu(left, right, dims):
    return lax.dot_general(left, right, dims, preferred_element_type=jnp.float32)


def regroup(parts):
    return [
        jnp.concatenate([part[:, 32 * group : 32 * group + 32] for part in parts], axis=1)
        for group in range(4)
    ]


def cos_sin(turns):
    quadrant = (turns + NLON // 8) >> 10
    angle = (turns - (quadrant << 10)).astype(jnp.float32) * (2.0 * math.pi / NLON)
    sq = angle * angle
    sin = angle * (
        1.0 + sq * (-1.0 / 6 + sq * (1.0 / 120 + sq * (-1.0 / 5040 + sq * (1.0 / 362880))))
    )
    cos = 1.0 + sq * (
        -0.5 + sq * (1.0 / 24 + sq * (-1.0 / 720 + sq * (1.0 / 40320 + sq * (-1.0 / 3628800))))
    )
    swap = (quadrant & 1) == 1
    first = jnp.where(swap, sin, cos)
    second = jnp.where(swap, cos, sin)
    turned = quadrant & 3
    cos_out = jnp.where((turned == 1) | (turned == 2), -first, first)
    sin_out = jnp.where(turned >= 2, -second, second)
    return (cos_out, sin_out)


def mean_decay(rate, decay):
    series = jnp.full_like(rate, 1.0 / math.factorial(11))
    for order in range(10, 0, -1):
        series = 1.0 / math.factorial(order) - rate * series
    return jnp.where(rate < 1.0, series, (1.0 - decay) / rate)


def forward_kernel(waves_ref, field_ref, out_ref, table_ref, folded):
    @pl.when(pl.program_id(0) == 0)
    def _():
        west = field_ref[:, :FOLD]
        east = field_ref[:, FOLD:]
        for parity, value in ((0, west + east), (1, west - east)):
            high, low = split(value)
            folded[parity, :128, :] = high
            folded[parity, 128:, :] = low

    lane = lax.broadcasted_iota(jnp.int32, (32, 128), 1)
    for parity in range(2):
        for start in range(0, PAIR_BLOCK, 32):
            rows = pl.ds(start, 32)
            wave = waves_ref[parity, rows, :]
            cos, sin = cos_sin((wave * lane) & (NLON - 1))
            turn_cos, turn_sin = cos_sin((wave * 128) & (NLON - 1))
            for block in range(FOLD // 128):
                cols = pl.ds(block * 128, 128)
                for component, value in ((0, cos), (1, -sin)):
                    high, low = split(value)
                    table_ref[0, parity, component, rows, cols] = high
                    table_ref[1, parity, component, rows, cols] = low
                cos, sin = (cos * turn_cos - sin * turn_sin, sin * turn_cos + cos * turn_sin)
    parts = []
    for parity in range(2):
        table = table_ref[:, parity].reshape(4 * PAIR_BLOCK, FOLD)
        product = mxu(table, folded[parity], NT)
        product = product[:, :128] + product[:, 128:]
        product = product[: 2 * PAIR_BLOCK] + product[2 * PAIR_BLOCK :]
        product = product * (1.0 / math.sqrt(NLON))
        parts += [product[:PAIR_BLOCK], product[PAIR_BLOCK:]]
    for level, value in enumerate(regroup(parts)):
        out_ref[pl.ds(level, PAIR_BLOCK, stride=4), :] = value


def forward(waves, field):
    return pl.pallas_call(
        forward_kernel,
        grid=(PAIRS // PAIR_BLOCK,),
        in_specs=[
            pl.BlockSpec((2, PAIR_BLOCK, 128), lambda i: (0, i, 0)),
            pl.BlockSpec((128, NLON), lambda i: (0, 0)),
        ],
        out_specs=[
            pl.BlockSpec((4 * PAIR_BLOCK, 128), lambda i: (i, 0)),
            pl.BlockSpec((2, 2, 2, PAIR_BLOCK, FOLD), lambda i: (0, 0, 0, i, 0)),
        ],
        out_shape=[
            jax.ShapeDtypeStruct((4 * PAIRS, 128), jnp.float32),
            jax.ShapeDtypeStruct((2, 2, 2, PAIRS, FOLD), jnp.bfloat16),
        ],
        scratch_shapes=[pltpu.VMEM((2, 256, FOLD), jnp.bfloat16)],
        compiler_params=pltpu.CompilerParams(vmem_limit_bytes=VMEM),
        name="forward",
    )(waves, field)


def mirrored(block):
    lane = lax.broadcasted_iota(jnp.int32, block.shape, 1)
    return jnp.take_along_axis(block, 127 - lane, axis=1)


def legendre_kernel(
    wave_ref,
    received_ref,
    panel_ref,
    spectral_ref,
    quad_ref,
    diffusion_ref,
    remap_ref,
    scale_ref,
    new_ref,
    out_ref,
    folded,
    panel_high,
    panel_low,
    total,
):
    step = pl.program_id(0)
    first = wave_ref[0]

    @pl.when(step == 0)
    def _():
        def latitudes(group):
            rows = [received_ref[(4 * group + q) * LEV : (4 * group + q + 1) * LEV, :] for q in range(4)]
            return jnp.concatenate(regroup(rows), axis=0)

        for group in range(HALF // 128):
            cols = slice(128 * group, 128 * group + 128)
            north = latitudes(group)
            south = mirrored(latitudes(15 - group))
            weight = quad_ref[:, cols]
            for parity, value in ((0, weight * (north + south)), (1, weight * (north - south))):
                high, low = split(value)
                folded[64 * parity : 64 * parity + 64, cols] = high
                folded[128 + 64 * parity : 192 + 64 * parity, cols] = low
        total[...] = jnp.zeros_like(total)

    row_down = step * ROW_BLOCK + lax.broadcasted_iota(jnp.int32, (ROW_BLOCK, 128), 0)
    for chunk in range(8):
        cols = slice(128 * chunk, 128 * chunk + 128)
        value = panel_ref[pl.ds(chunk, ROW_BLOCK, stride=8), :]
        high, low = split(jnp.where(row_down < ROWS, value, 0.0))
        panel_high[:, cols] = high
        panel_low[:, cols] = low

    row = step * ROW_BLOCK + lax.broadcasted_iota(jnp.int32, (1, ROW_BLOCK), 1)
    leading = row < NTRUNC - first
    degree = jnp.where(leading, first + row, row - 1).astype(jnp.float32)
    parity = jnp.where(leading, row, row + first) & 1
    slot = jnp.where(leading, first & 1, 1 - (first & 1))
    combination = 2 * parity + slot
    inside = row < ROWS

    products = mxu(folded[...], panel_high[...], NT) + mxu(folded[...], panel_low[...], NT)
    products = products[:128] + products[128:]
    forcing = products[96:]
    for index in range(3):
        forcing = jnp.where(combination == index, products[32 * index : 32 * index + 32], forcing)

    rate = diffusion_ref[...] * (0.1 + degree * (degree + 1.0) / (NTRUNC * (NTRUNC + 1.0)))
    decay = jnp.exp(-rate)
    gain = mean_decay(rate, decay)
    decay = jnp.concatenate([decay, decay], axis=0)
    gain = jnp.concatenate([gain, gain], axis=0)
    advanced = jnp.where(inside, decay * spectral_ref[...] + gain * forcing, 0.0)
    new_ref[...] = advanced

    mixed = lax.dot_general(
        remap_ref[...],
        advanced,
        NN,
        precision=lax.Precision.HIGHEST,
        preferred_element_type=jnp.float32,
    )
    spread = jnp.concatenate([jnp.where(combination == index, mixed, 0.0) for index in range(4)], axis=0)
    spread = jnp.concatenate(split(spread), axis=0)
    more = mxu(spread, panel_high[...], NN) + mxu(spread, panel_low[...], NN)

    @pl.when(step == 0)
    def _():
        total[...] = more

    @pl.when(step > 0)
    def _():
        total[...] = total[...] + more

    @pl.when(step == ROW_STEPS - 1)
    def _():
        scale = scale_ref[...]

        def store(group, value):
            parts = regroup([value[LEV * part : LEV * part + LEV] for part in range(4)])
            for q in range(4):
                out_ref[(4 * group + q) * LEV : (4 * group + q + 1) * LEV, :] = parts[q]

        for group in range(HALF // 128):
            cols = slice(128 * group, 128 * group + 128)
            values = total[:128, cols] + total[128:, cols]
            even = values[:64] * scale
            odd = values[64:] * scale
            store(group, even + odd)
            store(15 - group, mirrored(even - odd))


def legendre(first_wave, received, panel, spectral, quad_weights, diffusion, remap, scale):
    whole = lambda shape: pl.BlockSpec(shape, lambda i: (0,) * len(shape))
    return pl.pallas_call(
        legendre_kernel,
        grid=(ROW_STEPS,),
        in_specs=[
            pl.BlockSpec(memory_space=pltpu.SMEM),
            whole((4 * PAIRS, 128)),
            pl.BlockSpec((8 * ROW_BLOCK, 128), lambda i: (i, 0)),
            pl.BlockSpec((2 * LEV, ROW_BLOCK), lambda i: (0, i)),
            whole((1, HALF)),
            whole((LEV, 1)),
            whole((2 * LEV, 2 * LEV)),
            whole((64, 1)),
        ],
        out_specs=[
            pl.BlockSpec((2 * LEV, ROW_BLOCK), lambda i: (0, i)),
            whole((4 * PAIRS, 128)),
        ],
        out_shape=[
            jax.ShapeDtypeStruct((2 * LEV, ROWS), jnp.float32),
            jax.ShapeDtypeStruct((4 * PAIRS, 128), jnp.float32),
        ],
        scratch_shapes=[
            pltpu.VMEM((256, HALF), jnp.bfloat16),
            pltpu.VMEM((ROW_BLOCK, HALF), jnp.bfloat16),
            pltpu.VMEM((ROW_BLOCK, HALF), jnp.bfloat16),
            pltpu.VMEM((256, HALF), jnp.float32),
        ],
        compiler_params=pltpu.CompilerParams(vmem_limit_bytes=VMEM),
        name="legendre",
    )(first_wave, received, panel, spectral, quad_weights, diffusion, remap, scale)


def inverse_kernel(received_ref, table_ref, out_ref, turned):
    step = pl.program_id(0)

    @pl.when(step == 0)
    def _():
        parts = regroup([received_ref[pl.ds(level, PAIRS, stride=4), :] for level in range(4)])
        for index, part in enumerate(parts):
            parity, component = divmod(index, 2)
            high, low = split(part.T)
            cols = slice(PAIRS * component, PAIRS * component + PAIRS)
            turned[parity, :128, cols] = high
            turned[parity, 128:, cols] = low

    halves = []
    for parity in range(2):
        left = turned[parity]
        product = mxu(left, table_ref[0, parity].reshape(2 * PAIRS, LON_BLOCK), NN)
        product += mxu(left, table_ref[1, parity].reshape(2 * PAIRS, LON_BLOCK), NN)
        halves.append(product[:128] + product[128:])
    start = pl.multiple_of(step * LON_BLOCK, LON_BLOCK)
    out_ref[:, pl.ds(start, LON_BLOCK)] = halves[0] + halves[1]
    out_ref[:, pl.ds(start + FOLD, LON_BLOCK)] = halves[0] - halves[1]


def inverse(received, table):
    return pl.pallas_call(
        inverse_kernel,
        grid=(FOLD // LON_BLOCK,),
        in_specs=[
            pl.BlockSpec((4 * PAIRS, 128), lambda i: (0, 0)),
            pl.BlockSpec((2, 2, 2, PAIRS, LON_BLOCK), lambda i: (0, 0, 0, 0, i)),
        ],
        out_specs=pl.BlockSpec((128, NLON), lambda i: (0, 0)),
        out_shape=jax.ShapeDtypeStruct((128, NLON), jnp.float32),
        scratch_shapes=[pltpu.VMEM((2, 256, 2 * PAIRS), jnp.bfloat16)],
        compiler_params=pltpu.CompilerParams(vmem_limit_bytes=VMEM),
        name="inverse",
    )(received, table)


def remap_matrix(bounds):
    lower = bounds[:, :1]
    upper = bounds[:, 1:]
    source = jnp.arange(LEV, dtype=jnp.int32)[None, :]
    crossing = jnp.minimum(upper, (source + 1) * SUBDIV) - jnp.maximum(lower, source * SUBDIV)
    weights = jnp.maximum(crossing, 0).astype(jnp.float32) / (upper - lower).astype(jnp.float32)
    empty = jnp.zeros_like(weights)
    return jnp.block([[weights, empty], [empty, weights]])


def exchange(block):
    moved = lax.all_to_all(block.reshape(PAIRS, 4, 128), ("lat", "lev"), 0, 0, tiled=True)
    return moved.reshape(4 * PAIRS, 128)


def body(tendency, spectral, panel, quad_weights, diffusion, waves, bounds):
    own_pair = lax.axis_index("lat") * lax.axis_size("lev") + lax.axis_index("lev")
    odd = waves % 2
    even_odd = jnp.stack([jnp.where(odd == 1, NTRUNC - 1 - waves, waves), jnp.where(odd == 1, waves, NTRUNC - 1 - waves)])
    wave_rows = jnp.broadcast_to(even_odd[:, :, None], (2, PAIRS, 128))
    first_wave = lax.dynamic_slice_in_dim(waves, own_pair, 1)
    even_scale = jnp.where(first_wave == 0, 1.0, 2.0).astype(jnp.float32)
    odd_scale = jnp.full((1,), 2.0, jnp.float32)
    scale = jnp.repeat(jnp.concatenate([even_scale, odd_scale]), 2 * LEV)[:, None] / math.sqrt(NLON)

    coeffs, table = forward(wave_rows, tendency.reshape(128, NLON))
    advanced, returned = legendre(
        first_wave,
        exchange(coeffs),
        panel.reshape(8 * ROWS, 128),
        spectral.reshape(2 * LEV, ROWS),
        quad_weights[None, :],
        diffusion[:, None],
        remap_matrix(bounds),
        scale,
    )
    grid = inverse(exchange(returned), table)
    return (grid.reshape(tendency.shape), advanced.reshape(spectral.shape))


def solution(mesh):
    return jax.shard_map(
        body,
        mesh=mesh,
        in_specs=(
            P("lev", "lat", None),
            P(("lat", "lev"), None, None, None),
            P(("lat", "lev"), None, None),
            P(),
            P(),
            P(),
            P(),
        ),
        out_specs=(P("lev", "lat", None), P(("lat", "lev"), None, None, None)),
        check_vma=False,
    )
```

profile of v0, /device:TPU:1, one launch (start us, length us, event | category | flops | bytes accessed | tf_op | source)
XLA Modules:
  0.0 106.3 jit_solution(3420571736704293086)
XLA Ops:
  0.6 0.7 subtract_select_fusion.1
  1.3 0.8 broadcast_in_dim.12.waves_ref
  2.2 9.6 %forward.1 = (f32[1024,128]{1,0:T(8,128)}, bf16[2,2,2,256,2048]{4,3,2,1,0:T(8,128)(2,1)}) custom-call(s32[2,256,128]{2,1,0:T(8,128)} %broadcast_in_dim.12.waves_ref, f32[128,4096]{1,0:T(8,128)} %bitcast.21), custom_call_target="tpu_custom_call" | custom-call | tf_op jit(solution)/shard_map/forward/pallas_call | solution.py:107
  11.8 15.7 %all-to-all-start = ((f32[256,4,128]{2,1,0:T(4,128)}), f32[256,4,128]{2,1,0:T(4,128)S(1)}, u32[]{:S(2)}, u32[]{:S(2)}) async-start(f32[256,4,128]{2,1,0:T(4,128)} %bitcast.24), calls=%async_computation | async-start | bytes 1048576 | tf_op jit(solution)/shard_map/all_to_all | solution.py:321
  27.4 1.3 %dynamic_slice.3.wave_ref = s32[1]{0:T(128)} dynamic-slice(s32[256]{0:T(256)} %param.12, s32[]{:T(128)S(6)} %select_n.21), dynamic_slice_sizes={1} | dynamic-slice | bytes 12 | tf_op jit(solution)/shard_map/dynamic_slice | solution.py:330
  28.8 1.3 %copy.9.diffusion_ref = f32[16,1]{1,0:T(8,128)} copy(f32[16,1]{0,1:T(1,128)} %bitcast.30) | data formatting | bytes 128 | tf_op jit(solution)/shard_map/broadcast_in_dim | solution.py:342
  30.8 0.1 maximum_multiply_fusion
  30.9 0.1 broadcast_in_dim.24
  30.9 0.7 div.24.scale_ref
  31.6 0.8 slice_bitcast_fusion.1
  32.4 0.1 convert_divide_fusion
  32.5 0.7 select_maximum_fusion.remap_ref
  33.2 15.5 %all-to-all-done = f32[256,4,128]{2,1,0:T(4,128)S(1)} async-done(((f32[256,4,128]{2,1,0:T(4,128)}), f32[256,4,128]{2,1,0:T(4,128)S(1)}, u32[]{:S(2)}, u32[]{:S(2)}) %all-to-all-start) | async-done | bytes 524320 | tf_op jit(solution)/shard_map/all_to_all | solution.py:321
  48.7 0.0 copy-start
  48.7 0.8 copy-done
  49.5 20.9 %legendre.1 = (f32[32,2049]{1,0:T(8,128)}, f32[1024,128]{1,0:T(8,128)}) custom-call(s32[1]{0:T(128)} %dynamic_slice.3.wave_ref, f32[1024,128]{1,0:T(8,128)} %bitcast.20, f32[16392,128]{1,0:T(8,128)} %bitcast.19, f32[32,2049]{1,0:T(8,128)} %bitcast.26, f32[1,1024]{1,0:T(1,128)} %bitcast.27, f32[16,1]{1,0:T(8,128)} %copy.9.diffusion_ref, ...), custom_call_target="tpu_custom_call" | custom-call | tf_op jit(solution)/shard_map/legendre/pallas_call | solution.py:238
  70.4 28.3 %all_to_all.10 = f32[256,4,128]{2,1,0:T(4,128)} all-to-all(f32[256,4,128]{2,1,0:T(4,128)} %bitcast.25), channel_id=1, replica_groups=mesh['lat'=64,'lev'=4] {'lat','lev'}, dimensions={0} | all-to-all | bytes 1048576 | tf_op jit(solution)/shard_map/all_to_all | solution.py:321
  98.7 7.6 %inverse.1 = f32[128,4096]{1,0:T(8,128)} custom-call(f32[1024,128]{1,0:T(8,128)} %bitcast.23, bf16[2,2,2,256,2048]{4,3,2,1,0:T(8,128)(2,1)} %get-tuple-element.8.table_ref), custom_call_target="tpu_custom_call" | custom-call | tf_op jit(solution)/shard_map/inverse/pallas_call | solution.py:295
  (2 shorter events, 0.0 us)
Async XLA Ops:
  11.8 36.9 %all-to-all-start = ((f32[256,4,128]{2,1,0:T(4,128)}), f32[256,4,128]{2,1,0:T(4,128)S(1)}, u32[]{:S(2)}, u32[]{:S(2)}) async-start(f32[256,4,128]{2,1,0:T(4,128)} %bitcast.24), calls=%async_computation | async-start | bytes 1048576 | tf_op jit(solution)/shard_map/all_to_all | solution.py:321
  48.7 0.8 copy-start
where the time goes:
time: 107 us; the launch traced here: 106 us
  Pallas kernels  38.1 us (36%)
  blocking collectives  28.3 us (26%)
  starting transfers between devices  15.7 us (15%)
  waiting for transfers between devices  15.5 us (14%)
  local copies, waits for them, and re-layouts  5.07 us (5%)
  other arithmetic  2.29 us (2%)
  between operations  1.34 us (1%)
    all_to_all x1, blocking collectives, exchange(): lax.all_to_all(block.reshape(PAIRS, 4, 128), ('lat', 'lev'), 0, 0, tiled=...  28.3 us
    pallas_call x1, Pallas kernels, legendre(): pl.pallas_call(legendre_kernel, grid=(ROW_STEPS,), in_specs=[pl.BlockSpec...  20.9 us
    all_to_all x1, starting transfers between devices, exchange(): lax.all_to_all(block.reshape(PAIRS, 4, 128), ('lat', 'lev'), 0, 0, tiled=...  15.7 us
    all_to_all x1, waiting for transfers between devices, exchange(): lax.all_to_all(block.reshape(PAIRS, 4, 128), ('lat', 'lev'), 0, 0, tiled=...  15.5 us
    pallas_call x1, Pallas kernels, forward(): pl.pallas_call(forward_kernel, grid=(PAIRS // PAIR_BLOCK,), in_specs=[pl....  9.6 us
    pallas_call x1, Pallas kernels, inverse(): pl.pallas_call(inverse_kernel, grid=(FOLD // LON_BLOCK,), in_specs=[pl.Bl...  7.6 us
  transfers between devices with their start and end apart: 1, of which 1 were waited for; matrix products, arithmetic and copies ran while one was open for 5% of the time, Pallas kernels for 0%

commit v1 on v0

v1 whole, which is shorter than its diff:
```python
import math

import jax
import jax.numpy as jnp
from jax import lax
from jax.experimental import pallas as pl
from jax.experimental.pallas import tpu as pltpu
from jax.sharding import PartitionSpec as P

NTRUNC = 2048
SUBDIV = 8
NLON = 4096
TURN = 2 * NLON
FOLD = NLON // 2
QUARTER = NLON // 4
PAIRS = 256
ROWS = 2049
HALF = 1024
LEV = 16
ROW_BLOCK = 256
ROWS_PAD = 2176
CHUNKS = (0, 512, 1024, 1536, ROWS_PAD)
ROW_STEPS = -(-ROWS // ROW_BLOCK)
LON_BLOCK = 512
VMEM = 58 * 1024 * 1024
NT = (((1,), (1,)), ((), ()))
NN = (((1,), (0,)), ((), ()))


def split(value):
    high = value.astype(jnp.bfloat16)
    low = (value - high.astype(jnp.float32)).astype(jnp.bfloat16)
    return (high, low)


def mxu(left, right, dims):
    return lax.dot_general(left, right, dims, preferred_element_type=jnp.float32)


def regroup(parts):
    return [
        jnp.concatenate([part[:, 32 * group : 32 * group + 32] for part in parts], axis=1)
        for group in range(4)
    ]


def cos_sin(turns):
    quadrant = (turns + TURN // 8) >> 11
    angle = (turns - (quadrant << 11)).astype(jnp.float32) * (2.0 * math.pi / TURN)
    sq = angle * angle
    sin = angle * (
        1.0 + sq * (-1.0 / 6 + sq * (1.0 / 120 + sq * (-1.0 / 5040 + sq * (1.0 / 362880))))
    )
    cos = 1.0 + sq * (
        -0.5 + sq * (1.0 / 24 + sq * (-1.0 / 720 + sq * (1.0 / 40320 + sq * (-1.0 / 3628800))))
    )
    swap = (quadrant & 1) == 1
    first = jnp.where(swap, sin, cos)
    second = jnp.where(swap, cos, sin)
    turned = quadrant & 3
    cos_out = jnp.where((turned == 1) | (turned == 2), -first, first)
    sin_out = jnp.where(turned >= 2, -second, second)
    return (cos_out, sin_out)


def mirrored(block):
    lane = lax.broadcasted_iota(jnp.int32, block.shape, 1)
    return jnp.take_along_axis(block, 127 - lane, axis=1)


def mirrored_wide(block):
    width = block.shape[1]
    parts = [mirrored(block[:, start - 128 : start]) for start in range(width, 0, -128)]
    return jnp.concatenate(parts, axis=1)


def wave_columns(waves_ref):
    halves = []
    for half in range(PAIRS // 128):
        row = waves_ref[half : half + 1, :].astype(jnp.float32)
        halves.append(jnp.broadcast_to(row, (128, 128)).T.astype(jnp.int32))
    wave = jnp.concatenate(halves, axis=0)
    even = jnp.where((wave & 1) == 1, NTRUNC - 1 - wave, wave)
    return (even, NTRUNC - 1 - even)


def mean_decay(rate, decay):
    series = jnp.full_like(rate, 1.0 / math.factorial(11))
    for order in range(10, 0, -1):
        series = 1.0 / math.factorial(order) - rate * series
    return jnp.where(rate < 1.0, series, (1.0 - decay) / rate)


def forward_kernel(waves_ref, field_hbm, out_ref, table_hbm, field, folded, table, sems):
    load = pltpu.make_async_copy(field_hbm, field, sems.at[2])
    load.start()
    waves = wave_columns(waves_ref)
    lane = lax.broadcasted_iota(jnp.int32, (32, 128), 1)
    half_steps = [[], []]

    def build(parity):
        for start in range(0, PAIRS, 32):
            rows = slice(start, start + 32)
            wave = waves[parity][rows]
            half_cos, half_sin = cos_sin(wave)
            half_steps[parity].append((half_cos, half_sin))
            cos, sin = cos_sin((wave * (2 * lane + 1)) & (TURN - 1))
            last_cos = jnp.broadcast_to(cos[:, 127:], cos.shape)
            last_sin = jnp.broadcast_to(sin[:, 127:], sin.shape)
            turn_cos = last_cos * half_cos - last_sin * half_sin
            turn_sin = last_sin * half_cos + last_cos * half_sin
            for block in range(QUARTER // 128):
                cols = slice(block * 128, block * 128 + 128)
                for component, value in ((0, cos), (1, -sin)):
                    high, low = split(value)
                    table[parity, component, 0, rows, cols] = high
                    table[parity, component, 1, rows, cols] = low
                cos, sin = (cos * turn_cos - sin * turn_sin, sin * turn_cos + cos * turn_sin)

    def store(parity):
        return pltpu.make_async_copy(table.at[parity], table_hbm.at[parity], sems.at[parity])

    build(0)
    store(0).start()
    load.wait()
    for start in range(0, QUARTER, 128):
        near = slice(start, start + 128)
        far = slice(FOLD - 128 - start, FOLD - start)
        west_near, west_far = field[:, near], field[:, far]
        east_near = field[:, start + FOLD : start + FOLD + 128]
        east_far = field[:, NLON - 128 - start : NLON - start]
        for parity in range(2):
            sign = 1.0 - 2.0 * parity
            head = west_near + sign * east_near
            tail = mirrored(west_far + sign * east_far)
            for component, value in ((parity, head + tail), (1 - parity, head - tail)):
                high, low = split(value)
                folded[parity, component, :128, near] = high
                folded[parity, component, 128:, near] = low
    parts = []
    for parity in range(2):
        if parity == 1:
            build(1)
            store(1).start()
        sums = []
        for component in range(2):
            left = table[parity, component].reshape(2 * PAIRS, QUARTER)
            product = mxu(left, folded[parity, component], NT)
            product = product[:, :128] + product[:, 128:]
            sums.append((product[:PAIRS] + product[PAIRS:]) * (1.0 / math.sqrt(NLON)))
        half_cos = jnp.concatenate([item[0] for item in half_steps[parity]], axis=0)
        half_sin = jnp.concatenate([item[1] for item in half_steps[parity]], axis=0)
        parts += [sums[0] * half_cos - sums[1] * half_sin, sums[0] * half_sin + sums[1] * half_cos]
    for level, value in enumerate(regroup(parts)):
        out_ref[pl.ds(level, PAIRS, stride=4), :] = value
    for parity in range(2):
        store(parity).wait()


def forward(waves, field):
    return pl.pallas_call(
        forward_kernel,
        in_specs=[pl.BlockSpec(memory_space=pltpu.VMEM), pl.BlockSpec(memory_space=pl.ANY)],
        out_specs=[pl.BlockSpec(memory_space=pltpu.VMEM), pl.BlockSpec(memory_space=pl.ANY)],
        out_shape=[
            jax.ShapeDtypeStruct((4 * PAIRS, 128), jnp.float32),
            jax.ShapeDtypeStruct((2, 2, 2, PAIRS, QUARTER), jnp.bfloat16),
        ],
        scratch_shapes=[
            pltpu.VMEM((128, NLON), jnp.float32),
            pltpu.VMEM((2, 2, 256, QUARTER), jnp.bfloat16),
            pltpu.VMEM((2, 2, 2, PAIRS, QUARTER), jnp.bfloat16),
            pltpu.SemaphoreType.DMA((3,)),
        ],
        compiler_params=pltpu.CompilerParams(vmem_limit_bytes=VMEM),
        name="forward",
    )(waves, field)


def row_layout(first, row):
    leading = row < NTRUNC - first
    degree = jnp.where(leading, first + row, row - 1).astype(jnp.float32)
    parity = jnp.where(leading, row, row + first) & 1
    slot = jnp.where(leading, first & 1, 1 - (first & 1))
    return (degree, 2 * parity + slot)


def prepare_kernel(wave_ref, panel_ref, diffusion_ref, high_ref, low_ref, decay_ref, gain_ref):
    step = pl.program_id(0)
    row_down = step * ROW_BLOCK + lax.broadcasted_iota(jnp.int32, (ROW_BLOCK, 128), 0)
    for chunk in range(8):
        cols = slice(128 * chunk, 128 * chunk + 128)
        value = panel_ref[pl.ds(chunk, ROW_BLOCK, stride=8), :]
        high, low = split(jnp.where(row_down < ROWS, value, 0.0))
        high_ref[:, cols] = high
        low_ref[:, cols] = low
    row = step * ROW_BLOCK + lax.broadcasted_iota(jnp.int32, (1, ROW_BLOCK), 1)
    degree, _ = row_layout(wave_ref[0], row)
    rate = diffusion_ref[...] * (0.1 + degree * (degree + 1.0) / (NTRUNC * (NTRUNC + 1.0)))
    decay = jnp.exp(-rate)
    decay_ref[...] = decay
    gain_ref[...] = mean_decay(rate, decay)


def prepare(first_wave, panel, diffusion):
    rows = ROW_STEPS * ROW_BLOCK
    by_rows = pl.BlockSpec((ROW_BLOCK, HALF), lambda i: (i, 0))
    by_cols = pl.BlockSpec((LEV, ROW_BLOCK), lambda i: (0, i))
    return pl.pallas_call(
        prepare_kernel,
        grid=(ROW_STEPS,),
        in_specs=[
            pl.BlockSpec(memory_space=pltpu.SMEM),
            pl.BlockSpec((8 * ROW_BLOCK, 128), lambda i: (i, 0)),
            pl.BlockSpec((LEV, 1), lambda i: (0, 0)),
        ],
        out_specs=[by_rows, by_rows, by_cols, by_cols],
        out_shape=[
            jax.ShapeDtypeStruct((rows, HALF), jnp.bfloat16),
            jax.ShapeDtypeStruct((rows, HALF), jnp.bfloat16),
            jax.ShapeDtypeStruct((LEV, rows), jnp.float32),
            jax.ShapeDtypeStruct((LEV, rows), jnp.float32),
        ],
        compiler_params=pltpu.CompilerParams(vmem_limit_bytes=VMEM),
        cost_estimate=pl.CostEstimate(flops=20_000_000, bytes_accessed=18_000_000, transcendentals=50_000),
        name="prepare",
    )(first_wave, panel, diffusion)


def legendre_kernel(
    wave_ref,
    received_ref,
    high_hbm,
    low_hbm,
    spectral_ref,
    quad_ref,
    decay_ref,
    gain_ref,
    remap_ref,
    scale_ref,
    new_ref,
    out_ref,
    folded,
    panel_high,
    panel_low,
    spread,
    sems,
):
    first = wave_ref[0]
    loads = []
    for index, start in enumerate(CHUNKS[:-1]):
        rows = pl.ds(start, CHUNKS[index + 1] - start)
        for kind, (source, target) in enumerate(((high_hbm, panel_high), (low_hbm, panel_low))):
            loads.append(
                pltpu.make_async_copy(source.at[rows, :], target.at[rows, :], sems.at[index, kind])
            )
            loads[-1].start()

    def latitudes(group):
        rows = [received_ref[(4 * group + q) * LEV : (4 * group + q + 1) * LEV, :] for q in range(4)]
        return jnp.concatenate(regroup(rows), axis=0)

    for group in range(HALF // 128):
        cols = slice(128 * group, 128 * group + 128)
        north = latitudes(group)
        south = mirrored(latitudes(15 - group))
        weight = quad_ref[:, cols]
        for parity, value in ((0, weight * (north + south)), (1, weight * (north - south))):
            high, low = split(value)
            folded[64 * parity : 64 * parity + 64, cols] = high
            folded[128 + 64 * parity : 192 + 64 * parity, cols] = low

    weight_high, weight_low = split(remap_ref[...])
    weights = jnp.concatenate([weight_high, weight_high, weight_low], axis=1)
    for index, start in enumerate(CHUNKS[:-1]):
        stop = CHUNKS[index + 1]
        rows = slice(start, stop)
        row = start + lax.broadcasted_iota(jnp.int32, (1, stop - start), 1)
        _, combination = row_layout(first, row)
        loads[2 * index].wait()
        loads[2 * index + 1].wait()
        products = mxu(folded[...], panel_high[rows, :], NT) + mxu(folded[...], panel_low[rows, :], NT)
        products = products[:128] + products[128:]
        forcing = products[96:]
        for group in range(3):
            forcing = jnp.where(combination == group, products[32 * group : 32 * group + 32], forcing)
        decay = decay_ref[:, rows]
        gain = gain_ref[:, rows]
        advanced = (
            jnp.concatenate([decay, decay], axis=0) * spectral_ref[:, rows]
            + jnp.concatenate([gain, gain], axis=0) * forcing
        )
        stop = min(stop, ROWS)
        new_ref[:, start:stop] = advanced[:, : stop - start]
        high, low = split(advanced)
        mixed = mxu(weights, jnp.concatenate([high, low, high], axis=0), NN)
        for part, value in enumerate(split(mixed)):
            zero = jnp.zeros_like(value)
            for group in range(4):
                place = slice(128 * part + 32 * group, 128 * part + 32 * group + 32)
                spread[place, rows] = jnp.where(combination == group, value, zero)
    total = mxu(spread[...], panel_high[...], NN) + mxu(spread[...], panel_low[...], NN)
    total = total[:128] + total[128:]

    scale = scale_ref[...]

    def store(group, value):
        parts = regroup([value[LEV * part : LEV * part + LEV] for part in range(4)])
        for q in range(4):
            out_ref[(4 * group + q) * LEV : (4 * group + q + 1) * LEV, :] = parts[q]

    for group in range(HALF // 128):
        cols = slice(128 * group, 128 * group + 128)
        even = total[:64, cols] * scale
        odd = total[64:, cols] * scale
        store(group, even + odd)
        store(15 - group, mirrored(even - odd))


def legendre(first_wave, received, prepared, spectral, quad_weights, remap, scale):
    high, low, decay, gain = prepared
    vmem = pl.BlockSpec(memory_space=pltpu.VMEM)
    anywhere = pl.BlockSpec(memory_space=pl.ANY)
    return pl.pallas_call(
        legendre_kernel,
        in_specs=[pl.BlockSpec(memory_space=pltpu.SMEM), vmem, anywhere, anywhere] + [vmem] * 6,
        out_specs=[vmem, vmem],
        out_shape=[
            jax.ShapeDtypeStruct((2 * LEV, ROWS), jnp.float32),
            jax.ShapeDtypeStruct((4 * PAIRS, 128), jnp.float32),
        ],
        scratch_shapes=[
            pltpu.VMEM((256, HALF), jnp.bfloat16),
            pltpu.VMEM((ROWS_PAD, HALF), jnp.bfloat16),
            pltpu.VMEM((ROWS_PAD, HALF), jnp.bfloat16),
            pltpu.VMEM((256, ROWS_PAD), jnp.bfloat16),
            pltpu.SemaphoreType.DMA((len(CHUNKS) - 1, 2)),
        ],
        compiler_params=pltpu.CompilerParams(vmem_limit_bytes=VMEM),
        name="legendre",
    )(first_wave, received, high, low, spectral, quad_weights, decay, gain, remap, scale)


def inverse_kernel(waves_ref, received_ref, table_hbm, out_hbm, turned, table, grid, load_sems, store_sems):
    count = QUARTER // LON_BLOCK

    def load(parity):
        return pltpu.make_async_copy(table_hbm.at[parity], table.at[parity], load_sems.at[parity])

    def store(index, part):
        begin = (
            index * LON_BLOCK,
            FOLD - (index + 1) * LON_BLOCK,
            FOLD + index * LON_BLOCK,
            NLON - (index + 1) * LON_BLOCK,
        )[part]
        cols = pl.ds(begin, LON_BLOCK)
        return pltpu.make_async_copy(grid.at[:, cols], out_hbm.at[:, cols], store_sems.at[index, part])

    load(0).start()
    load(1).start()
    waves = wave_columns(waves_ref)
    parts = regroup([received_ref[pl.ds(level, PAIRS, stride=4), :] for level in range(4)])
    for parity in range(2):
        half_cos, half_sin = cos_sin(waves[parity])
        real, imag = parts[2 * parity], parts[2 * parity + 1]
        for component, value in (
            (0, real * half_cos + imag * half_sin),
            (1, imag * half_cos - real * half_sin),
        ):
            high, low = split(value.T)
            for copy in range(2):
                cols = slice(PAIRS * copy, PAIRS * copy + PAIRS)
                turned[parity, component, :128, cols] = high
                turned[parity, component, 128:, cols] = low
    for index in range(count):
        cols = slice(index * LON_BLOCK, index * LON_BLOCK + LON_BLOCK)
        near, far = [], []
        for parity in range(2):
            if index == 0:
                load(parity).wait()
            sums = []
            for component in range(2):
                right = table[parity, component, :, :, cols].reshape(2 * PAIRS, LON_BLOCK)
                product = mxu(turned[parity, component], right, NN)
                sums.append(product[:128] + product[128:])
            near.append(sums[0] + sums[1])
            far.append(sums[parity] - sums[1 - parity])
        for part, value in enumerate(
            (
                near[0] + near[1],
                mirrored_wide(far[0] + far[1]),
                near[0] - near[1],
                mirrored_wide(far[0] - far[1]),
            )
        ):
            begin = (
                index * LON_BLOCK,
                FOLD - (index + 1) * LON_BLOCK,
                FOLD + index * LON_BLOCK,
                NLON - (index + 1) * LON_BLOCK,
            )[part]
            grid[:, begin : begin + LON_BLOCK] = value
            store(index, part).start()
    for index in range(count):
        for part in range(4):
            store(index, part).wait()


def inverse(waves, received, table):
    vmem = pl.BlockSpec(memory_space=pltpu.VMEM)
    return pl.pallas_call(
        inverse_kernel,
        in_specs=[vmem, vmem, pl.BlockSpec(memory_space=pl.ANY)],
        out_specs=pl.BlockSpec(memory_space=pl.ANY),
        out_shape=jax.ShapeDtypeStruct((128, NLON), jnp.float32),
        scratch_shapes=[
            pltpu.VMEM((2, 2, 256, 2 * PAIRS), jnp.bfloat16),
            pltpu.VMEM((2, 2, 2, PAIRS, QUARTER), jnp.bfloat16),
            pltpu.VMEM((128, NLON), jnp.float32),
            pltpu.SemaphoreType.DMA((2,)),
            pltpu.SemaphoreType.DMA((QUARTER // LON_BLOCK, 4)),
        ],
        compiler_params=pltpu.CompilerParams(vmem_limit_bytes=VMEM),
        name="inverse",
    )(waves, received, table)


def remap_matrix(bounds):
    lower = bounds[:, :1]
    upper = bounds[:, 1:]
    source = jnp.arange(LEV, dtype=jnp.int32)[None, :]
    crossing = jnp.minimum(upper, (source + 1) * SUBDIV) - jnp.maximum(lower, source * SUBDIV)
    weights = jnp.maximum(crossing, 0).astype(jnp.float32) / (upper - lower).astype(jnp.float32)
    empty = jnp.zeros_like(weights)
    return jnp.block([[weights, empty], [empty, weights]])


def exchange(block):
    moved = lax.all_to_all(block.reshape(PAIRS, 4, 128), ("lat", "lev"), 0, 0, tiled=True)
    return moved.reshape(4 * PAIRS, 128)


def body(tendency, spectral, panel, quad_weights, diffusion, waves, bounds):
    own_pair = lax.axis_index("lat") * lax.axis_size("lev") + lax.axis_index("lev")
    wave_rows = waves.reshape(PAIRS // 128, 128)
    first_wave = lax.dynamic_slice_in_dim(waves, own_pair, 1)
    even_scale = jnp.where(first_wave == 0, 1.0, 2.0).astype(jnp.float32)
    odd_scale = jnp.full((1,), 2.0, jnp.float32)
    scale = jnp.repeat(jnp.concatenate([even_scale, odd_scale]), 2 * LEV)[:, None] / math.sqrt(NLON)

    coeffs, table = forward(wave_rows, tendency.reshape(128, NLON))
    spectral_rows = jnp.pad(spectral.reshape(2 * LEV, ROWS), ((0, 0), (0, ROWS_PAD - ROWS)))
    advanced, returned = legendre(
        first_wave,
        exchange(coeffs),
        prepare(first_wave, panel.reshape(8 * ROWS, 128), diffusion[:, None]),
        spectral_rows,
        quad_weights[None, :],
        remap_matrix(bounds),
        scale,
    )
    grid = inverse(wave_rows, exchange(returned), table)
    return (grid.reshape(tendency.shape), advanced.reshape(spectral.shape))


def solution(mesh):
    return jax.shard_map(
        body,
        mesh=mesh,
        in_specs=(
            P("lev", "lat", None),
            P(("lat", "lev"), None, None, None),
            P(("lat", "lev"), None, None),
            P(),
            P(),
            P(),
            P(),
        ),
        out_specs=(P("lev", "lat", None), P(("lat", "lev"), None, None, None)),
        check_vma=False,
    )
```

time: 107 us -> 94.6 us (0.88)
  waiting for transfers between devices: 15.5 us -> 3.06 us
  blocking collectives: 28.3 us -> 32 us
  Pallas kernels: 38.1 us -> 35.1 us
  other arithmetic: 2.29 us -> 0.84 us
    all_to_all x1, waiting for transfers between devices: 15.5 us -> 3.06 us  [exchange(): lax.all_to_all(block.reshape(PAIRS, 4, 128), ('lat', 'lev'), 0, 0, tiled=...]
    all_to_all x1, blocking collectives: 28.3 us -> 32 us  [exchange(): lax.all_to_all(block.reshape(PAIRS, 4, 128), ('lat', 'lev'), 0, 0, tiled=...]
    pallas_call x3 -> x4, Pallas kernels: 38.1 us -> 35.1 us  [the longest x1 11.5 us: prepare(): pl.pallas_call(prepare_kernel, grid=(ROW_STEPS,), in_specs=[pl.BlockSpec(...]
    pad x0 -> x1, local copies, waits for them, and re-layouts: none -> 1.67 us  [body(): jnp.pad(spectral.reshape(2 * LEV, ROWS), ((0, 0), (0, ROWS_PAD - ROWS)))]
  transfers between devices with their start and end apart: 1 -> 1, of which waited for: 1 -> 1; matrix products, arithmetic and copies ran while one was open for 5% -> 6% of each run, Pallas kernels for 0% -> 12%
where the time goes in v1:
time: 94.6 us; the launch traced here: 94.1 us
  Pallas kernels  35.1 us (37%)
  blocking collectives  32 us (34%)
  starting transfers between devices  15.7 us (17%)
  local copies, waits for them, and re-layouts  5.92 us (6%)
  waiting for transfers between devices  3.06 us (3%)
  between operations  1.55 us (2%)
    all_to_all x1, blocking collectives, exchange(): lax.all_to_all(block.reshape(PAIRS, 4, 128), ('lat', 'lev'), 0, 0, tiled=...  32 us
    all_to_all x1, starting transfers between devices, exchange(): lax.all_to_all(block.reshape(PAIRS, 4, 128), ('lat', 'lev'), 0, 0, tiled=...  15.7 us
    pallas_call x1, Pallas kernels, prepare(): pl.pallas_call(prepare_kernel, grid=(ROW_STEPS,), in_specs=[pl.BlockSpec(...  11.5 us
    pallas_call x1, Pallas kernels, legendre(): pl.pallas_call(legendre_kernel, in_specs=[pl.BlockSpec(memory_space=pltpu...  11.3 us
    pallas_call x1, Pallas kernels, forward(): pl.pallas_call(forward_kernel, in_specs=[pl.BlockSpec(memory_space=pltpu....  6.79 us
    pallas_call x1, Pallas kernels, inverse(): pl.pallas_call(inverse_kernel, in_specs=[vmem, vmem, pl.BlockSpec(memory_...  5.47 us
    all_to_all x1, waiting for transfers between devices, exchange(): lax.all_to_all(block.reshape(PAIRS, 4, 128), ('lat', 'lev'), 0, 0, tiled=...  3.06 us
  transfers between devices with their start and end apart: 1, of which 1 were waited for; matrix products, arithmetic and copies ran while one was open for 6% of the time, Pallas kernels for 12%

profile of v1, /device:TPU:1, one launch (start us, length us, event | category | flops | bytes accessed | tf_op | source)
XLA Modules:
  0.0 94.1 jit_solution(18308650091475743247)
XLA Ops:
  0.6 6.8 %forward.1 = (f32[1024,128]{1,0:T(8,128)}, bf16[2,2,2,256,1024]{4,3,2,1,0:T(8,128)(2,1)}) custom-call(s32[2,128]{1,0:T(2,128)} %bitcast.27, f32[128,4096]{1,0:T(8,128)} %bitcast.21), custom_call_target="tpu_custom_call" | custom-call | tf_op jit(solution)/shard_map/forward/pallas_call | solution.py:161
  7.4 15.7 %all-to-all-start = ((f32[256,4,128]{2,1,0:T(4,128)}), f32[256,4,128]{2,1,0:T(4,128)S(1)}, u32[]{:S(2)}, u32[]{:S(2)}) async-start(f32[256,4,128]{2,1,0:T(4,128)} %bitcast.23), calls=%async_computation | async-start | bytes 1048576 | tf_op jit(solution)/shard_map/all_to_all | solution.py:440
  23.1 0.0 copy-start.1
  23.1 1.3 %dynamic_slice.3.wave_ref = s32[1]{0:T(128)} dynamic-slice(s32[256]{0:T(256)} %param.12, s32[]{:T(128)S(6)} %select_n.7), dynamic_slice_sizes={1} | dynamic-slice | bytes 12 | tf_op jit(solution)/shard_map/dynamic_slice | solution.py:447
  24.5 1.3 %copy.9.diffusion_ref = f32[16,1]{1,0:T(8,128)} copy(f32[16,1]{0,1:T(1,128)} %bitcast.29) | data formatting | bytes 128 | tf_op jit(solution)/shard_map/broadcast_in_dim | solution.py:457
  26.5 0.1 maximum_multiply_fusion
  26.6 0.1 broadcast_in_dim.17
  26.6 0.7 div.24.scale_ref
  27.4 1.7 %pad.6.spectral_ref = f32[32,2176]{1,0:T(8,128)} pad(f32[32,2049]{1,0:T(8,128)} %bitcast.25, f32[]{:T(128)} %constant.11.clone.1), padding=0_0x0_127 | pad | bytes 540804 | tf_op jit(solution)/shard_map/jit(_pad)/pad | solution.py:453
  29.0 11.5 %prepare.1 = (bf16[2304,1024]{1,0:T(8,128)(2,1)}, bf16[2304,1024]{1,0:T(8,128)(2,1)}, f32[16,2304]{1,0:T(8,128)}, f32[16,2304]{1,0:T(8,128)}) custom-call(s32[1]{0:T(128)} %dynamic_slice.3.wave_ref, f32[16392,128]{1,0:T(8,128)} %bitcast.18, f32[16,1]{1,0:T(8,128)} %copy.9.diffusion_ref), custom_call_target="tpu_custom_call" | custom-call | flops 20000000 | bytes 18000000 | tf_op jit(solution)/shard_map/prepare/pallas_call | solution.py:209
  40.5 0.0 copy-done.1
  40.5 0.1 convert_divide_fusion
  40.6 0.7 select_maximum_fusion.remap_ref
  41.3 3.1 %all-to-all-done = f32[256,4,128]{2,1,0:T(4,128)S(1)} async-done(((f32[256,4,128]{2,1,0:T(4,128)}), f32[256,4,128]{2,1,0:T(4,128)S(1)}, u32[]{:S(2)}, u32[]{:S(2)}) %all-to-all-start) | async-done | bytes 524320 | tf_op jit(solution)/shard_map/all_to_all | solution.py:440
  44.3 0.0 copy-start
  44.3 0.8 copy-done
  45.1 11.3 %legendre.1 = (f32[32,2049]{1,0:T(8,128)}, f32[1024,128]{1,0:T(8,128)}) custom-call(s32[1]{0:T(128)} %dynamic_slice.3.wave_ref, f32[1024,128]{1,0:T(8,128)} %bitcast.19, bf16[2304,1024]{1,0:T(8,128)(2,1)} %get-tuple-element.11.high_hbm, bf16[2304,1024]{1,0:T(8,128)(2,1)} %get-tuple-element.12.low_hbm, f32[32,2176]{1,0:T(8,128)} %pad.6.spectral_ref, ...), custom_call_target="tpu_custom_call" | custom-call | tf_op jit(solution)/shard_map/legendre/pallas_call | solution.py:324
  56.5 32.0 %all_to_all.10 = f32[256,4,128]{2,1,0:T(4,128)} all-to-all(f32[256,4,128]{2,1,0:T(4,128)} %bitcast.24), channel_id=1, replica_groups=mesh['lat'=64,'lev'=4] {'lat','lev'}, dimensions={0} | all-to-all | bytes 1048576 | tf_op jit(solution)/shard_map/all_to_all | solution.py:440
  88.4 5.5 %inverse.1 = f32[128,4096]{1,0:T(8,128)} custom-call(s32[2,128]{1,0:T(2,128)} %bitcast.28, f32[1024,128]{1,0:T(8,128)} %bitcast.20, bf16[2,2,2,256,1024]{4,3,2,1,0:T(8,128)(2,1)} %get-tuple-element.16.table_hbm), custom_call_target="tpu_custom_call" | custom-call | tf_op jit(solution)/shard_map/inverse/pallas_call | solution.py:412
  (2 shorter events, 0.0 us)
Async XLA Ops:
  7.4 36.9 %all-to-all-start = ((f32[256,4,128]{2,1,0:T(4,128)}), f32[256,4,128]{2,1,0:T(4,128)S(1)}, u32[]{:S(2)}, u32[]{:S(2)}) async-start(f32[256,4,128]{2,1,0:T(4,128)} %bitcast.23), calls=%async_computation | async-start | bytes 1048576 | tf_op jit(solution)/shard_map/all_to_all | solution.py:440
  23.1 17.4 %copy-start.1 = (s32[16,2]{0,1:T(2,128)S(1)}, s32[16,2]{0,1:T(2,128)}, u32[]{:S(2)}) copy-start(s32[16,2]{0,1:T(2,128)} %param.13) | copy-start | bytes 388
  44.3 0.8 copy-start

commit v2 on v1

--- a/solution.py
+++ b/solution.py
@@ -17,11 +17,10 @@
 ROWS = 2049
 HALF = 1024
 LEV = 16
-ROW_BLOCK = 256
+ROW_BLOCK = 512
 ROWS_PAD = 2176
-CHUNKS = (0, 512, 1024, 1536, ROWS_PAD)
-ROW_STEPS = -(-ROWS // ROW_BLOCK)
-LON_BLOCK = 512
+CHUNKS = (0, 1024, ROWS_PAD)
+LON_CUTS = (0, 512, 768, 1024)
 VMEM = 58 * 1024 * 1024
 NT = (((1,), (1,)), ((), ()))
 NN = (((1,), (0,)), ((), ()))
@@ -91,9 +90,20 @@
     return jnp.where(rate < 1.0, series, (1.0 - decay) / rate)
 
 
-def forward_kernel(waves_ref, field_hbm, out_ref, table_hbm, field, folded, table, sems):
-    load = pltpu.make_async_copy(field_hbm, field, sems.at[2])
-    load.start()
+def forward_kernel(
+    waves_hbm, field_hbm, out_ref, table_hbm, waves_ref, field, folded, table, sems, load_sems
+):
+    loads = []
+    for index in range(4):
+        rows = pl.ds(32 * index, 32)
+        loads.append(
+            pltpu.make_async_copy(field_hbm.at[rows, :], field.at[rows, :], load_sems.at[index])
+        )
+    load_waves = pltpu.make_async_copy(waves_hbm, waves_ref, sems.at[2])
+    load_waves.start()
+    for load in loads:
+        load.start()
+    load_waves.wait()
     waves = wave_columns(waves_ref)
     lane = lax.broadcasted_iota(jnp.int32, (32, 128), 1)
     half_steps = [[], []]
@@ -120,28 +130,27 @@
     def store(parity):
         return pltpu.make_async_copy(table.at[parity], table_hbm.at[parity], sems.at[parity])
 
-    build(0)
-    store(0).start()
-    load.wait()
-    for start in range(0, QUARTER, 128):
-        near = slice(start, start + 128)
-        far = slice(FOLD - 128 - start, FOLD - start)
-        west_near, west_far = field[:, near], field[:, far]
-        east_near = field[:, start + FOLD : start + FOLD + 128]
-        east_far = field[:, NLON - 128 - start : NLON - start]
-        for parity in range(2):
-            sign = 1.0 - 2.0 * parity
-            head = west_near + sign * east_near
-            tail = mirrored(west_far + sign * east_far)
+    for parity in range(2):
+        build(parity)
+        store(parity).start()
+    for load in loads:
+        load.wait()
+    parts = []
+    for parity in range(2):
+        for start in range(0, QUARTER, 128):
+            near = slice(start, start + 128)
+            head, tail = field[:, near], field[:, FOLD - 128 - start : FOLD - start]
+            east_head = field[:, start + FOLD : start + FOLD + 128]
+            east_tail = field[:, NLON - 128 - start : NLON - start]
+            if parity == 0:
+                head, tail = head + east_head, tail + east_tail
+            else:
+                head, tail = head - east_head, tail - east_tail
+            tail = mirrored(tail)
             for component, value in ((parity, head + tail), (1 - parity, head - tail)):
                 high, low = split(value)
                 folded[parity, component, :128, near] = high
                 folded[parity, component, 128:, near] = low
-    parts = []
-    for parity in range(2):
-        if parity == 1:
-            build(1)
-            store(1).start()
         sums = []
         for component in range(2):
             left = table[parity, component].reshape(2 * PAIRS, QUARTER)
@@ -160,17 +169,19 @@
 def forward(waves, field):
     return pl.pallas_call(
         forward_kernel,
-        in_specs=[pl.BlockSpec(memory_space=pltpu.VMEM), pl.BlockSpec(memory_space=pl.ANY)],
+        in_specs=[pl.BlockSpec(memory_space=pl.ANY)] * 2,
         out_specs=[pl.BlockSpec(memory_space=pltpu.VMEM), pl.BlockSpec(memory_space=pl.ANY)],
         out_shape=[
             jax.ShapeDtypeStruct((4 * PAIRS, 128), jnp.float32),
             jax.ShapeDtypeStruct((2, 2, 2, PAIRS, QUARTER), jnp.bfloat16),
         ],
         scratch_shapes=[
+            pltpu.VMEM((PAIRS // 128, 128), jnp.int32),
             pltpu.VMEM((128, NLON), jnp.float32),
             pltpu.VMEM((2, 2, 256, QUARTER), jnp.bfloat16),
             pltpu.VMEM((2, 2, 2, PAIRS, QUARTER), jnp.bfloat16),
             pltpu.SemaphoreType.DMA((3,)),
+            pltpu.SemaphoreType.DMA((4,)),
         ],
         compiler_params=pltpu.CompilerParams(vmem_limit_bytes=VMEM),
         name="forward",
@@ -185,68 +196,108 @@
     return (degree, 2 * parity + slot)
 
 
-def prepare_kernel(wave_ref, panel_ref, diffusion_ref, high_ref, low_ref, decay_ref, gain_ref):
+def own_wave(waves_ref):
+    return waves_ref[lax.axis_index("lat") * lax.axis_size("lev") + lax.axis_index("lev")]
+
+
+def column(values_ref, shape):
+    row = lax.broadcasted_iota(jnp.int32, shape, 0) % LEV
+    result = jnp.full(shape, values_ref[0])
+    for index in range(1, LEV):
+        result = jnp.where(row == index, values_ref[index], result)
+    return result
+
+
+def prepare_kernel(waves_ref, diffusion_ref, panel_ref, high_ref, low_ref, decay_ref, gain_ref):
     step = pl.program_id(0)
-    row_down = step * ROW_BLOCK + lax.broadcasted_iota(jnp.int32, (ROW_BLOCK, 128), 0)
-    for chunk in range(8):
-        cols = slice(128 * chunk, 128 * chunk + 128)
-        value = panel_ref[pl.ds(chunk, ROW_BLOCK, stride=8), :]
-        high, low = split(jnp.where(row_down < ROWS, value, 0.0))
-        high_ref[:, cols] = high
-        low_ref[:, cols] = low
-    row = step * ROW_BLOCK + lax.broadcasted_iota(jnp.int32, (1, ROW_BLOCK), 1)
-    degree, _ = row_layout(wave_ref[0], row)
-    rate = diffusion_ref[...] * (0.1 + degree * (degree + 1.0) / (NTRUNC * (NTRUNC + 1.0)))
-    decay = jnp.exp(-rate)
-    decay_ref[...] = decay
-    gain_ref[...] = mean_decay(rate, decay)
-
-
-def prepare(first_wave, panel, diffusion):
-    rows = ROW_STEPS * ROW_BLOCK
+    last = ROWS // ROW_BLOCK
+
+    def divide(rows, keep):
+        for chunk in range(8):
+            cols = slice(128 * chunk, 128 * chunk + 128)
+            high, low = split(keep(panel_ref[pl.ds(chunk, rows, stride=8), :]))
+            high_ref[:rows, cols] = high
+            low_ref[:rows, cols] = low
+        row = step * ROW_BLOCK + lax.broadcasted_iota(jnp.int32, (1, rows), 1)
+        degree, _ = row_layout(own_wave(waves_ref), row)
+        scaled = 0.1 + degree * (degree + 1.0) / (NTRUNC * (NTRUNC + 1.0))
+        rate = column(diffusion_ref, (LEV, rows)) * scaled
+        decay = jnp.exp(-rate)
+        decay_ref[:, :rows] = decay
+        gain_ref[:, :rows] = mean_decay(rate, decay)
+
+    @pl.when(step < last)
+    def _():
+        divide(ROW_BLOCK, lambda value: value)
+
+    @pl.when(step == last)
+    def _():
+        rows = ROWS_PAD - last * ROW_BLOCK
+        inside = lax.broadcasted_iota(jnp.int32, (rows, 128), 0) < ROWS - last * ROW_BLOCK
+        divide(rows, lambda value: jnp.where(inside, value, 0.0))
+
+
+def prepare(waves, panel, diffusion):
     by_rows = pl.BlockSpec((ROW_BLOCK, HALF), lambda i: (i, 0))
     by_cols = pl.BlockSpec((LEV, ROW_BLOCK), lambda i: (0, i))
     return pl.pallas_call(
         prepare_kernel,
-        grid=(ROW_STEPS,),
+        grid=(ROWS // ROW_BLOCK + 1,),
         in_specs=[
             pl.BlockSpec(memory_space=pltpu.SMEM),
+            pl.BlockSpec(memory_space=pltpu.SMEM),
             pl.BlockSpec((8 * ROW_BLOCK, 128), lambda i: (i, 0)),
-            pl.BlockSpec((LEV, 1), lambda i: (0, 0)),
         ],
         out_specs=[by_rows, by_rows, by_cols, by_cols],
         out_shape=[
-            jax.ShapeDtypeStruct((rows, HALF), jnp.bfloat16),
-            jax.ShapeDtypeStruct((rows, HALF), jnp.bfloat16),
-            jax.ShapeDtypeStruct((LEV, rows), jnp.float32),
-            jax.ShapeDtypeStruct((LEV, rows), jnp.float32),
+            jax.ShapeDtypeStruct((ROWS_PAD, HALF), jnp.bfloat16),
+            jax.ShapeDtypeStruct((ROWS_PAD, HALF), jnp.bfloat16),
+            jax.ShapeDtypeStruct((LEV, ROWS_PAD), jnp.float32),
+            jax.ShapeDtypeStruct((LEV, ROWS_PAD), jnp.float32),
         ],
         compiler_params=pltpu.CompilerParams(vmem_limit_bytes=VMEM),
         cost_estimate=pl.CostEstimate(flops=20_000_000, bytes_accessed=18_000_000, transcendentals=50_000),
         name="prepare",
-    )(first_wave, panel, diffusion)
+    )(waves, diffusion, panel)
+
+
+def remap_matrix(bounds_ref):
+    shape = (2 * LEV, 2 * LEV)
+    target = lax.broadcasted_iota(jnp.int32, shape, 0)
+    source = lax.broadcasted_iota(jnp.int32, shape, 1)
+    lower = column(bounds_ref.at[0], shape)
+    upper = column(bounds_ref.at[1], shape)
+    level = source % LEV
+    crossing = jnp.minimum(upper, (level + 1) * SUBDIV) - jnp.maximum(lower, level * SUBDIV)
+    crossing = jnp.where(target // LEV == source // LEV, jnp.maximum(crossing, 0), 0)
+    return crossing.astype(jnp.float32) / (upper - lower).astype(jnp.float32)
 
 
 def legendre_kernel(
-    wave_ref,
+    waves_ref,
+    bounds_ref,
     received_ref,
     high_hbm,
     low_hbm,
-    spectral_ref,
-    quad_ref,
-    decay_ref,
-    gain_ref,
-    remap_ref,
-    scale_ref,
-    new_ref,
+    spectral_hbm,
+    quad_hbm,
+    decay_hbm,
+    gain_hbm,
+    new_hbm,
     out_ref,
     folded,
     panel_high,
     panel_low,
     spread,
+    spectral_ref,
+    quad_ref,
+    decay_ref,
+    gain_ref,
+    tail,
+    new_ref,
     sems,
+    small_sems,
 ):
-    first = wave_ref[0]
     loads = []
     for index, start in enumerate(CHUNKS[:-1]):
         rows = pl.ds(start, CHUNKS[index + 1] - start)
@@ -254,7 +305,27 @@
             loads.append(
                 pltpu.make_async_copy(source.at[rows, :], target.at[rows, :], sems.at[index, kind])
             )
-            loads[-1].start()
+    small = [
+        pltpu.make_async_copy(source, target, small_sems.at[index])
+        for index, (source, target) in enumerate(
+            (
+                (quad_hbm, quad_ref),
+                (spectral_hbm, spectral_ref),
+                (decay_hbm, decay_ref),
+                (gain_hbm, gain_ref),
+            )
+        )
+    ]
+    small[0].start()
+    loads[0].start()
+    loads[1].start()
+    for copy in small[1:] + loads[2:]:
+        copy.start()
+    first = own_wave(waves_ref)
+    tail[...] = jnp.zeros_like(tail)
+    weight_high, weight_low = split(remap_matrix(bounds_ref))
+    weights = jnp.concatenate([weight_high, weight_high, weight_low], axis=1)
+    small[0].wait()
 
     def latitudes(group):
         rows = [received_ref[(4 * group + q) * LEV : (4 * group + q + 1) * LEV, :] for q in range(4)]
@@ -270,8 +341,6 @@
             folded[64 * parity : 64 * parity + 64, cols] = high
             folded[128 + 64 * parity : 192 + 64 * parity, cols] = low
 
-    weight_high, weight_low = split(remap_ref[...])
-    weights = jnp.concatenate([weight_high, weight_high, weight_low], axis=1)
     for index, start in enumerate(CHUNKS[:-1]):
         stop = CHUNKS[index + 1]
         rows = slice(start, stop)
@@ -284,10 +353,17 @@
         forcing = products[96:]
         for group in range(3):
             forcing = jnp.where(combination == group, products[32 * group : 32 * group + 32], forcing)
+        if index == 0:
+            for copy in small[1:]:
+                copy.wait()
+            tail[:, :1] = spectral_ref[:, ROWS - 1 :]
         decay = decay_ref[:, rows]
         gain = gain_ref[:, rows]
+        state = spectral_ref[:, start : min(stop, ROWS - 1)]
+        if stop > ROWS:
+            state = jnp.concatenate([state, tail[...]], axis=1)
         advanced = (
-            jnp.concatenate([decay, decay], axis=0) * spectral_ref[:, rows]
+            jnp.concatenate([decay, decay], axis=0) * state
             + jnp.concatenate([gain, gain], axis=0) * forcing
         )
         stop = min(stop, ROWS)
@@ -299,10 +375,13 @@
             for group in range(4):
                 place = slice(128 * part + 32 * group, 128 * part + 32 * group + 32)
                 spread[place, rows] = jnp.where(combination == group, value, zero)
-    total = mxu(spread[...], panel_high[...], NN) + mxu(spread[...], panel_low[...], NN)
-    total = total[:128] + total[128:]
-
-    scale = scale_ref[...]
+    store_new = pltpu.make_async_copy(new_ref, new_hbm, small_sems.at[4])
+    store_new.start()
+    total = mxu(spread[...], panel_high[...], NN)
+    total = total[:128] + total[128:] + mxu(spread[:128], panel_low[...], NN)
+
+    slot = lax.broadcasted_iota(jnp.int32, (64, 128), 0) // (2 * LEV)
+    scale = jnp.where((slot == 0) & (first == 0), 1.0, 2.0) / math.sqrt(NLON)
 
     def store(group, value):
         parts = regroup([value[LEV * part : LEV * part + LEV] for part in range(4)])
@@ -315,16 +394,18 @@
         odd = total[64:, cols] * scale
         store(group, even + odd)
         store(15 - group, mirrored(even - odd))
-
-
-def legendre(first_wave, received, prepared, spectral, quad_weights, remap, scale):
+    store_new.wait()
+
+
+def legendre(waves, bounds, received, prepared, spectral, quad_weights):
     high, low, decay, gain = prepared
     vmem = pl.BlockSpec(memory_space=pltpu.VMEM)
+    smem = pl.BlockSpec(memory_space=pltpu.SMEM)
     anywhere = pl.BlockSpec(memory_space=pl.ANY)
     return pl.pallas_call(
         legendre_kernel,
-        in_specs=[pl.BlockSpec(memory_space=pltpu.SMEM), vmem, anywhere, anywhere] + [vmem] * 6,
-        out_specs=[vmem, vmem],
+        in_specs=[smem, smem, vmem] + [anywhere] * 6,
+        out_specs=[anywhere, vmem],
         out_shape=[
             jax.ShapeDtypeStruct((2 * LEV, ROWS), jnp.float32),
             jax.ShapeDtypeStruct((4 * PAIRS, 128), jnp.float32),
@@ -334,33 +415,45 @@
             pltpu.VMEM((ROWS_PAD, HALF), jnp.bfloat16),
             pltpu.VMEM((ROWS_PAD, HALF), jnp.bfloat16),
             pltpu.VMEM((256, ROWS_PAD), jnp.bfloat16),
+            pltpu.VMEM((2 * LEV, ROWS), jnp.float32),
+            pltpu.VMEM((1, HALF), jnp.float32),
+            pltpu.VMEM((LEV, ROWS_PAD), jnp.float32),
+            pltpu.VMEM((LEV, ROWS_PAD), jnp.float32),
+            pltpu.VMEM((2 * LEV, 128), jnp.float32),
+            pltpu.VMEM((2 * LEV, ROWS), jnp.float32),
             pltpu.SemaphoreType.DMA((len(CHUNKS) - 1, 2)),
+            pltpu.SemaphoreType.DMA((5,)),
         ],
         compiler_params=pltpu.CompilerParams(vmem_limit_bytes=VMEM),
         name="legendre",
-    )(first_wave, received, high, low, spectral, quad_weights, decay, gain, remap, scale)
-
-
-def inverse_kernel(waves_ref, received_ref, table_hbm, out_hbm, turned, table, grid, load_sems, store_sems):
-    count = QUARTER // LON_BLOCK
+    )(waves, bounds, received, high, low, spectral, quad_weights, decay, gain)
+
+
+def inverse_kernel(
+    waves_hbm, received_ref, table_hbm, out_hbm, waves_ref, turned, table, grid, load_sems, store_sems
+):
+    count = len(LON_CUTS) - 1
 
     def load(parity):
         return pltpu.make_async_copy(table_hbm.at[parity], table.at[parity], load_sems.at[parity])
 
+    def target(index, part):
+        start, stop = LON_CUTS[index], LON_CUTS[index + 1]
+        begin = (start, FOLD - stop, FOLD + start, NLON - stop)[part]
+        return slice(begin, begin + stop - start)
+
     def store(index, part):
-        begin = (
-            index * LON_BLOCK,
-            FOLD - (index + 1) * LON_BLOCK,
-            FOLD + index * LON_BLOCK,
-            NLON - (index + 1) * LON_BLOCK,
-        )[part]
-        cols = pl.ds(begin, LON_BLOCK)
+        cols = target(index, part)
+        cols = pl.ds(cols.start, cols.stop - cols.start)
         return pltpu.make_async_copy(grid.at[:, cols], out_hbm.at[:, cols], store_sems.at[index, part])
 
-    load(0).start()
-    load(1).start()
+    load_waves = pltpu.make_async_copy(waves_hbm, waves_ref, load_sems.at[2])
+    load_waves.start()
+    for parity in range(2):
+        load(parity).start()
+    parts = regroup([received_ref[pl.ds(level, PAIRS, stride=4), :] for level in range(4)])
+    load_waves.wait()
     waves = wave_columns(waves_ref)
-    parts = regroup([received_ref[pl.ds(level, PAIRS, stride=4), :] for level in range(4)])
     for parity in range(2):
         half_cos, half_sin = cos_sin(waves[parity])
         real, imag = parts[2 * parity], parts[2 * parity + 1]
@@ -374,14 +467,14 @@
                 turned[parity, component, :128, cols] = high
                 turned[parity, component, 128:, cols] = low
     for index in range(count):
-        cols = slice(index * LON_BLOCK, index * LON_BLOCK + LON_BLOCK)
+        cols = slice(LON_CUTS[index], LON_CUTS[index + 1])
         near, far = [], []
         for parity in range(2):
             if index == 0:
                 load(parity).wait()
             sums = []
             for component in range(2):
-                right = table[parity, component, :, :, cols].reshape(2 * PAIRS, LON_BLOCK)
+                right = table[parity, component, :, :, cols].reshape(2 * PAIRS, cols.stop - cols.start)
                 product = mxu(turned[parity, component], right, NN)
                 sums.append(product[:128] + product[128:])
             near.append(sums[0] + sums[1])
@@ -394,13 +487,7 @@
                 mirrored_wide(far[0] - far[1]),
             )
         ):
-            begin = (
-                index * LON_BLOCK,
-                FOLD - (index + 1) * LON_BLOCK,
-                FOLD + index * LON_BLOCK,
-                NLON - (index + 1) * LON_BLOCK,
-            )[part]
-            grid[:, begin : begin + LON_BLOCK] = value
+            grid[:, target(index, part)] = value
             store(index, part).start()
     for index in range(count):
         for part in range(4):
@@ -411,54 +498,37 @@
     vmem = pl.BlockSpec(memory_space=pltpu.VMEM)
     return pl.pallas_call(
         inverse_kernel,
-        in_specs=[vmem, vmem, pl.BlockSpec(memory_space=pl.ANY)],
+        in_specs=[pl.BlockSpec(memory_space=pl.ANY), vmem, pl.BlockSpec(memory_space=pl.ANY)],
         out_specs=pl.BlockSpec(memory_space=pl.ANY),
         out_shape=jax.ShapeDtypeStruct((128, NLON), jnp.float32),
         scratch_shapes=[
+            pltpu.VMEM((PAIRS // 128, 128), jnp.int32),
             pltpu.VMEM((2, 2, 256, 2 * PAIRS), jnp.bfloat16),
             pltpu.VMEM((2, 2, 2, PAIRS, QUARTER), jnp.bfloat16),
             pltpu.VMEM((128, NLON), jnp.float32),
-            pltpu.SemaphoreType.DMA((2,)),
-            pltpu.SemaphoreType.DMA((QUARTER // LON_BLOCK, 4)),
+            pltpu.SemaphoreType.DMA((3,)),
+            pltpu.SemaphoreType.DMA((len(LON_CUTS) - 1, 4)),
         ],
         compiler_params=pltpu.CompilerParams(vmem_limit_bytes=VMEM),
         name="inverse",
     )(waves, received, table)
 
 
-def remap_matrix(bounds):
-    lower = bounds[:, :1]
-    upper = bounds[:, 1:]
-    source = jnp.arange(LEV, dtype=jnp.int32)[None, :]
-    crossing = jnp.minimum(upper, (source + 1) * SUBDIV) - jnp.maximum(lower, source * SUBDIV)
-    weights = jnp.maximum(crossing, 0).astype(jnp.float32) / (upper - lower).astype(jnp.float32)
-    empty = jnp.zeros_like(weights)
-    return jnp.block([[weights, empty], [empty, weights]])
-
-
 def exchange(block):
     moved = lax.all_to_all(block.reshape(PAIRS, 4, 128), ("lat", "lev"), 0, 0, tiled=True)
     return moved.reshape(4 * PAIRS, 128)
 
 
 def body(tendency, spectral, panel, quad_weights, diffusion, waves, bounds):
-    own_pair = lax.axis_index("lat") * lax.axis_size("lev") + lax.axis_index("lev")
     wave_rows = waves.reshape(PAIRS // 128, 128)
-    first_wave = lax.dynamic_slice_in_dim(waves, own_pair, 1)
-    even_scale = jnp.where(first_wave == 0, 1.0, 2.0).astype(jnp.float32)
-    odd_scale = jnp.full((1,), 2.0, jnp.float32)
-    scale = jnp.repeat(jnp.concatenate([even_scale, odd_scale]), 2 * LEV)[:, None] / math.sqrt(NLON)
-
     coeffs, table = forward(wave_rows, tendency.reshape(128, NLON))
-    spectral_rows = jnp.pad(spectral.reshape(2 * LEV, ROWS), ((0, 0), (0, ROWS_PAD - ROWS)))
     advanced, returned = legendre(
-        first_wave,
+        waves,
+        bounds.T,
         exchange(coeffs),
-        prepare(first_wave, panel.reshape(8 * ROWS, 128), diffusion[:, None]),
-        spectral_rows,
+        prepare(waves, panel.reshape(8 * ROWS, 128), diffusion),
+        spectral.reshape(2 * LEV, ROWS),
         quad_weights[None, :],
-        remap_matrix(bounds),
-        scale,
     )
     grid = inverse(wave_rows, exchange(returned), table)
     return (grid.reshape(tendency.shape), advanced.reshape(spectral.shape))

time: 94.6 us -> 88.5 us (0.936)
  waiting for transfers between devices: 3.06 us -> 12.1 us
  local copies, waits for them, and re-layouts: 5.92 us -> 0.79 us
  Pallas kernels: 35.1 us -> 30.2 us
  blocking collectives: 32 us -> 28.5 us
    all_to_all x1, waiting for transfers between devices: 3.06 us -> 12.1 us  [exchange(): lax.all_to_all(block.reshape(PAIRS, 4, 128), ('lat', 'lev'), 0, 0, tiled=...]
    pallas_call x4, Pallas kernels: 35.1 us -> 30.2 us  [the longest x1 9.9 us: legendre(): pl.pallas_call(legendre_kernel, in_specs=[smem, smem, vmem] + [anywhere]...]
    all_to_all x1, blocking collectives: 32 us -> 28.5 us  [exchange(): lax.all_to_all(block.reshape(PAIRS, 4, 128), ('lat', 'lev'), 0, 0, tiled=...]
    pad x1 -> x0, local copies, waits for them, and re-layouts: 1.67 us -> none  [body(): jnp.pad(spectral.reshape(2 * LEV, ROWS), ((0, 0), (0, ROWS_PAD - ROWS)))]
    broadcast_in_dim x2 -> x0, local copies, waits for them, and re-layouts: 1.4 us -> none  [the longest x1 1.33 us: body(): diffusion[:, None]]
    dynamic_slice x1 -> x0, local copies, waits for them, and re-layouts: 1.34 us -> none  [body(): first_wave = lax.dynamic_slice_in_dim(waves, own_pair, 1)]
  transfers between devices with their start and end apart: 1 -> 1, of which waited for: 1 -> 1; matrix products, arithmetic and copies ran while one was open for 6% -> 0% of each run, Pallas kernels for 12% -> 10%
where the time goes in v2:
time: 88.5 us; the launch traced here: 88.2 us
  Pallas kernels  30.2 us (34%)
  blocking collectives  28.5 us (32%)
  starting transfers between devices  15.7 us (18%)
  waiting for transfers between devices  12.1 us (14%)
    all_to_all x1, blocking collectives, exchange(): lax.all_to_all(block.reshape(PAIRS, 4, 128), ('lat', 'lev'), 0, 0, tiled=...  28.5 us
    all_to_all x1, starting transfers between devices, exchange(): lax.all_to_all(block.reshape(PAIRS, 4, 128), ('lat', 'lev'), 0, 0, tiled=...  15.7 us
    all_to_all x1, waiting for transfers between devices, exchange(): lax.all_to_all(block.reshape(PAIRS, 4, 128), ('lat', 'lev'), 0, 0, tiled=...  12.1 us
    pallas_call x1, Pallas kernels, legendre(): pl.pallas_call(legendre_kernel, in_specs=[smem, smem, vmem] + [anywhere]...  9.9 us
    pallas_call x1, Pallas kernels, prepare(): pl.pallas_call(prepare_kernel, grid=(ROWS // ROW_BLOCK + 1,), in_specs=[p...  9.09 us
    pallas_call x1, Pallas kernels, forward(): pl.pallas_call(forward_kernel, in_specs=[pl.BlockSpec(memory_space=pl.ANY...  5.93 us
    pallas_call x1, Pallas kernels, inverse(): pl.pallas_call(inverse_kernel, in_specs=[pl.BlockSpec(memory_space=pl.ANY...  5.32 us
  transfers between devices with their start and end apart: 1, of which 1 were waited for; matrix products, arithmetic and copies ran while one was open for 0% of the time, Pallas kernels for 10%

profile of v2, /device:TPU:1, one launch (start us, length us, event | category | flops | bytes accessed | tf_op | source)
XLA Modules:
  0.0 88.2 jit_solution(12109933558428216060)
XLA Ops:
  0.6 5.9 %forward.1 = (f32[1024,128]{1,0:T(8,128)}, bf16[2,2,2,256,1024]{4,3,2,1,0:T(8,128)(2,1)}) custom-call(s32[2,128]{1,0:T(2,128)} %bitcast.20, f32[128,4096]{1,0:T(8,128)} %bitcast.15), custom_call_target="tpu_custom_call" | custom-call | tf_op jit(solution)/shard_map/forward/pallas_call | solution.py:170
  6.6 15.7 %all-to-all-start = ((f32[256,4,128]{2,1,0:T(4,128)}), f32[256,4,128]{2,1,0:T(4,128)S(1)}, u32[]{:S(2)}, u32[]{:S(2)}) async-start(f32[256,4,128]{2,1,0:T(4,128)} %bitcast.17), calls=%async_computation | async-start | bytes 1048576 | tf_op jit(solution)/shard_map/all_to_all | solution.py:518
  22.2 9.1 %prepare.1 = (bf16[2176,1024]{1,0:T(8,128)(2,1)}, bf16[2176,1024]{1,0:T(8,128)(2,1)}, f32[16,2176]{1,0:T(8,128)}, f32[16,2176]{1,0:T(8,128)}) custom-call(s32[256]{0:T(256)} %waves_ref.3, f32[16]{0:T(128)} %diffusion_ref.1, f32[16392,128]{1,0:T(8,128)} %bitcast.12), custom_call_target="tpu_custom_call" | custom-call | flops 20000000 | bytes 18000000 | tf_op jit(solution)/shard_map/prepare/pallas_call | solution.py:243
  31.3 12.1 %all-to-all-done = f32[256,4,128]{2,1,0:T(4,128)S(1)} async-done(((f32[256,4,128]{2,1,0:T(4,128)}), f32[256,4,128]{2,1,0:T(4,128)S(1)}, u32[]{:S(2)}, u32[]{:S(2)}) %all-to-all-start) | async-done | bytes 524320 | tf_op jit(solution)/shard_map/all_to_all | solution.py:518
  43.5 0.0 copy-start
  43.5 0.8 copy-done
  44.3 9.9 %legendre.1 = (f32[32,2049]{1,0:T(8,128)}, f32[1024,128]{1,0:T(8,128)}) custom-call(s32[256]{0:T(256)} %waves_ref.3, s32[2,16]{1,0:T(2,128)} %bitcast.23, f32[1024,128]{1,0:T(8,128)} %bitcast.13, bf16[2176,1024]{1,0:T(8,128)(2,1)} %get-tuple-element.11.high_hbm, bf16[2176,1024]{1,0:T(8,128)(2,1)} %get-tuple-element.12.low_hbm, f32[32,2049]{1,0:T(8,128)} %bitcast.19, ...), custom_call_target="tpu_custom_call" | custom-call | tf_op jit(solution)/shard_map/legendre/pallas_call | solution.py:405
  54.2 28.5 %all_to_all.10 = f32[256,4,128]{2,1,0:T(4,128)} all-to-all(f32[256,4,128]{2,1,0:T(4,128)} %bitcast.18), channel_id=1, replica_groups=mesh['lat'=64,'lev'=4] {'lat','lev'}, dimensions={0} | all-to-all | bytes 1048576 | tf_op jit(solution)/shard_map/all_to_all | solution.py:518
  82.7 5.3 %inverse.1 = f32[128,4096]{1,0:T(8,128)} custom-call(s32[2,128]{1,0:T(2,128)} %bitcast.21, f32[1024,128]{1,0:T(8,128)} %bitcast.14, bf16[2,2,2,256,1024]{4,3,2,1,0:T(8,128)(2,1)} %get-tuple-element.16.table_hbm), custom_call_target="tpu_custom_call" | custom-call | tf_op jit(solution)/shard_map/inverse/pallas_call | solution.py:499
Async XLA Ops:
  6.6 36.9 %all-to-all-start = ((f32[256,4,128]{2,1,0:T(4,128)}), f32[256,4,128]{2,1,0:T(4,128)S(1)}, u32[]{:S(2)}, u32[]{:S(2)}) async-start(f32[256,4,128]{2,1,0:T(4,128)} %bitcast.17), calls=%async_computation | async-start | bytes 1048576 | tf_op jit(solution)/shard_map/all_to_all | solution.py:518
  43.5 0.8 copy-start

commit v3 on v2

--- a/solution.py
+++ b/solution.py
@@ -22,6 +22,8 @@
 CHUNKS = (0, 1024, ROWS_PAD)
 LON_CUTS = (0, 512, 768, 1024)
 VMEM = 58 * 1024 * 1024
+VMEM_LEGENDRE = 52 * 1024 * 1024
+VMEM_INVERSE = 48 * 1024 * 1024
 NT = (((1,), (1,)), ((), ()))
 NN = (((1,), (0,)), ((), ()))
 
@@ -91,18 +93,12 @@
 
 
 def forward_kernel(
-    waves_hbm, field_hbm, out_ref, table_hbm, waves_ref, field, folded, table, sems, load_sems
+    waves_hbm, field_hbm, out_ref, table_hbm, waves_ref, field, folded, table, sems
 ):
-    loads = []
-    for index in range(4):
-        rows = pl.ds(32 * index, 32)
-        loads.append(
-            pltpu.make_async_copy(field_hbm.at[rows, :], field.at[rows, :], load_sems.at[index])
-        )
+    load = pltpu.make_async_copy(field_hbm, field, sems.at[3])
     load_waves = pltpu.make_async_copy(waves_hbm, waves_ref, sems.at[2])
     load_waves.start()
-    for load in loads:
-        load.start()
+    load.start()
     load_waves.wait()
     waves = wave_columns(waves_ref)
     lane = lax.broadcasted_iota(jnp.int32, (32, 128), 1)
@@ -133,8 +129,7 @@
     for parity in range(2):
         build(parity)
         store(parity).start()
-    for load in loads:
-        load.wait()
+    load.wait()
     parts = []
     for parity in range(2):
         for start in range(0, QUARTER, 128):
@@ -180,7 +175,6 @@
             pltpu.VMEM((128, NLON), jnp.float32),
             pltpu.VMEM((2, 2, 256, QUARTER), jnp.bfloat16),
             pltpu.VMEM((2, 2, 2, PAIRS, QUARTER), jnp.bfloat16),
-            pltpu.SemaphoreType.DMA((3,)),
             pltpu.SemaphoreType.DMA((4,)),
         ],
         compiler_params=pltpu.CompilerParams(vmem_limit_bytes=VMEM),
@@ -208,7 +202,7 @@
     return result
 
 
-def prepare_kernel(waves_ref, diffusion_ref, panel_ref, high_ref, low_ref, decay_ref, gain_ref):
+def prepare_kernel(panel_ref, high_ref, low_ref):
     step = pl.program_id(0)
     last = ROWS // ROW_BLOCK
 
@@ -218,13 +212,6 @@
             high, low = split(keep(panel_ref[pl.ds(chunk, rows, stride=8), :]))
             high_ref[:rows, cols] = high
             low_ref[:rows, cols] = low
-        row = step * ROW_BLOCK + lax.broadcasted_iota(jnp.int32, (1, rows), 1)
-        degree, _ = row_layout(own_wave(waves_ref), row)
-        scaled = 0.1 + degree * (degree + 1.0) / (NTRUNC * (NTRUNC + 1.0))
-        rate = column(diffusion_ref, (LEV, rows)) * scaled
-        decay = jnp.exp(-rate)
-        decay_ref[:, :rows] = decay
-        gain_ref[:, :rows] = mean_decay(rate, decay)
 
     @pl.when(step < last)
     def _():
@@ -237,28 +224,21 @@
         divide(rows, lambda value: jnp.where(inside, value, 0.0))
 
 
-def prepare(waves, panel, diffusion):
+def prepare(panel):
     by_rows = pl.BlockSpec((ROW_BLOCK, HALF), lambda i: (i, 0))
-    by_cols = pl.BlockSpec((LEV, ROW_BLOCK), lambda i: (0, i))
     return pl.pallas_call(
         prepare_kernel,
         grid=(ROWS // ROW_BLOCK + 1,),
-        in_specs=[
-            pl.BlockSpec(memory_space=pltpu.SMEM),
-            pl.BlockSpec(memory_space=pltpu.SMEM),
-            pl.BlockSpec((8 * ROW_BLOCK, 128), lambda i: (i, 0)),
-        ],
-        out_specs=[by_rows, by_rows, by_cols, by_cols],
+        in_specs=[pl.BlockSpec((8 * ROW_BLOCK, 128), lambda i: (i, 0))],
+        out_specs=[by_rows, by_rows],
         out_shape=[
             jax.ShapeDtypeStruct((ROWS_PAD, HALF), jnp.bfloat16),
             jax.ShapeDtypeStruct((ROWS_PAD, HALF), jnp.bfloat16),
-            jax.ShapeDtypeStruct((LEV, ROWS_PAD), jnp.float32),
-            jax.ShapeDtypeStruct((LEV, ROWS_PAD), jnp.float32),
         ],
         compiler_params=pltpu.CompilerParams(vmem_limit_bytes=VMEM),
-        cost_estimate=pl.CostEstimate(flops=20_000_000, bytes_accessed=18_000_000, transcendentals=50_000),
+        cost_estimate=pl.CostEstimate(flops=20_000_000, bytes_accessed=18_000_000, transcendentals=0),
         name="prepare",
-    )(waves, diffusion, panel)
+    )(panel)
 
 
 def remap_matrix(bounds_ref):
@@ -276,13 +256,12 @@
 def legendre_kernel(
     waves_ref,
     bounds_ref,
+    diffusion_ref,
     received_ref,
     high_hbm,
     low_hbm,
     spectral_hbm,
     quad_hbm,
-    decay_hbm,
-    gain_hbm,
     new_hbm,
     out_ref,
     folded,
@@ -311,8 +290,6 @@
             (
                 (quad_hbm, quad_ref),
                 (spectral_hbm, spectral_ref),
-                (decay_hbm, decay_ref),
-                (gain_hbm, gain_ref),
             )
         )
     ]
@@ -325,6 +302,15 @@
     tail[...] = jnp.zeros_like(tail)
     weight_high, weight_low = split(remap_matrix(bounds_ref))
     weights = jnp.concatenate([weight_high, weight_high, weight_low], axis=1)
+    degree, _ = row_layout(first, lax.broadcasted_iota(jnp.int32, (1, ROWS_PAD), 1))
+    strength = column(diffusion_ref, (LEV, 128))
+    for start in range(0, ROWS_PAD, 128):
+        rows = slice(start, start + 128)
+        scaled = 0.1 + degree[:, rows] * (degree[:, rows] + 1.0) / (NTRUNC * (NTRUNC + 1.0))
+        rate = strength * scaled
+        decay = jnp.exp(-rate)
+        decay_ref[:, rows] = decay
+        gain_ref[:, rows] = mean_decay(rate, decay)
     small[0].wait()
 
     def latitudes(group):
@@ -375,7 +361,7 @@
             for group in range(4):
                 place = slice(128 * part + 32 * group, 128 * part + 32 * group + 32)
                 spread[place, rows] = jnp.where(combination == group, value, zero)
-    store_new = pltpu.make_async_copy(new_ref, new_hbm, small_sems.at[4])
+    store_new = pltpu.make_async_copy(new_ref, new_hbm, small_sems.at[2])
     store_new.start()
     total = mxu(spread[...], panel_high[...], NN)
     total = total[:128] + total[128:] + mxu(spread[:128], panel_low[...], NN)
@@ -397,14 +383,14 @@
     store_new.wait()
 
 
-def legendre(waves, bounds, received, prepared, spectral, quad_weights):
-    high, low, decay, gain = prepared
+def legendre(waves, bounds, diffusion, received, prepared, spectral, quad_weights):
+    high, low = prepared
     vmem = pl.BlockSpec(memory_space=pltpu.VMEM)
     smem = pl.BlockSpec(memory_space=pltpu.SMEM)
     anywhere = pl.BlockSpec(memory_space=pl.ANY)
     return pl.pallas_call(
         legendre_kernel,
-        in_specs=[smem, smem, vmem] + [anywhere] * 6,
+        in_specs=[smem, smem, smem, vmem] + [anywhere] * 4,
         out_specs=[anywhere, vmem],
         out_shape=[
             jax.ShapeDtypeStruct((2 * LEV, ROWS), jnp.float32),
@@ -422,20 +408,17 @@
             pltpu.VMEM((2 * LEV, 128), jnp.float32),
             pltpu.VMEM((2 * LEV, ROWS), jnp.float32),
             pltpu.SemaphoreType.DMA((len(CHUNKS) - 1, 2)),
-            pltpu.SemaphoreType.DMA((5,)),
+            pltpu.SemaphoreType.DMA((3,)),
         ],
-        compiler_params=pltpu.CompilerParams(vmem_limit_bytes=VMEM),
+        compiler_params=pltpu.CompilerParams(vmem_limit_bytes=VMEM_LEGENDRE),
         name="legendre",
-    )(waves, bounds, received, high, low, spectral, quad_weights, decay, gain)
+    )(waves, bounds, diffusion, received, high, low, spectral, quad_weights)
 
 
 def inverse_kernel(
-    waves_hbm, received_ref, table_hbm, out_hbm, waves_ref, turned, table, grid, load_sems, store_sems
+    waves_hbm, received_ref, table, out_hbm, waves_ref, turned, grid, load_sems, store_sems
 ):
     count = len(LON_CUTS) - 1
-
-    def load(parity):
-        return pltpu.make_async_copy(table_hbm.at[parity], table.at[parity], load_sems.at[parity])
 
     def target(index, part):
         start, stop = LON_CUTS[index], LON_CUTS[index + 1]
@@ -449,8 +432,6 @@
 
     load_waves = pltpu.make_async_copy(waves_hbm, waves_ref, load_sems.at[2])
     load_waves.start()
-    for parity in range(2):
-        load(parity).start()
     parts = regroup([received_ref[pl.ds(level, PAIRS, stride=4), :] for level in range(4)])
     load_waves.wait()
     waves = wave_columns(waves_ref)
@@ -470,8 +451,6 @@
         cols = slice(LON_CUTS[index], LON_CUTS[index + 1])
         near, far = [], []
         for parity in range(2):
-            if index == 0:
-                load(parity).wait()
             sums = []
             for component in range(2):
                 right = table[parity, component, :, :, cols].reshape(2 * PAIRS, cols.stop - cols.start)
@@ -498,18 +477,17 @@
     vmem = pl.BlockSpec(memory_space=pltpu.VMEM)
     return pl.pallas_call(
         inverse_kernel,
-        in_specs=[pl.BlockSpec(memory_space=pl.ANY), vmem, pl.BlockSpec(memory_space=pl.ANY)],
+        in_specs=[pl.BlockSpec(memory_space=pl.ANY), vmem, vmem],
         out_specs=pl.BlockSpec(memory_space=pl.ANY),
         out_shape=jax.ShapeDtypeStruct((128, NLON), jnp.float32),
         scratch_shapes=[
             pltpu.VMEM((PAIRS // 128, 128), jnp.int32),
             pltpu.VMEM((2, 2, 256, 2 * PAIRS), jnp.bfloat16),
-            pltpu.VMEM((2, 2, 2, PAIRS, QUARTER), jnp.bfloat16),
             pltpu.VMEM((128, NLON), jnp.float32),
             pltpu.SemaphoreType.DMA((3,)),
             pltpu.SemaphoreType.DMA((len(LON_CUTS) - 1, 4)),
         ],
-        compiler_params=pltpu.CompilerParams(vmem_limit_bytes=VMEM),
+        compiler_params=pltpu.CompilerParams(vmem_limit_bytes=VMEM_INVERSE),
         name="inverse",
     )(waves, received, table)
 
@@ -525,8 +503,9 @@
     advanced, returned = legendre(
         waves,
         bounds.T,
+        diffusion,
         exchange(coeffs),
-        prepare(waves, panel.reshape(8 * ROWS, 128), diffusion),
+        prepare(panel.reshape(8 * ROWS, 128)),
         spectral.reshape(2 * LEV, ROWS),
         quad_weights[None, :],
     )

time: 88.5 us -> 83.1 us (0.939)
  Pallas kernels: 30.2 us -> 27 us
  blocking collectives: 28.5 us -> 27 us
    pallas_call x1, Pallas kernels: 5.32 us -> 3.32 us  [inverse(): pl.pallas_call(inverse_kernel, in_specs=[pl.BlockSpec(memory_space=pl.ANY...]
    all_to_all x1, blocking collectives: 28.5 us -> 27 us  [exchange(): lax.all_to_all(block.reshape(PAIRS, 4, 128), ('lat', 'lev'), 0, 0, tiled=...]
  transfers between devices with their start and end apart: 1 -> 1, of which waited for: 1 -> 1; matrix products, arithmetic and copies ran while one was open for 0% -> 0% of each run, Pallas kernels for 10% -> 11%
where the time goes in v3:
time: 83.1 us; the launch traced here: 82.9 us
  Pallas kernels  27 us (32%)
  blocking collectives  27 us (32%)
  starting transfers between devices  15.7 us (19%)
  waiting for transfers between devices  12.4 us (15%)
  between operations  0.88 us (1%)
    all_to_all x1, blocking collectives, exchange(): lax.all_to_all(block.reshape(PAIRS, 4, 128), ('lat', 'lev'), 0, 0, tiled=...  27 us
    all_to_all x1, starting transfers between devices, exchange(): lax.all_to_all(block.reshape(PAIRS, 4, 128), ('lat', 'lev'), 0, 0, tiled=...  15.7 us
    all_to_all x1, waiting for transfers between devices, exchange(): lax.all_to_all(block.reshape(PAIRS, 4, 128), ('lat', 'lev'), 0, 0, tiled=...  12.4 us
    pallas_call x1, Pallas kernels, legendre(): pl.pallas_call(legendre_kernel, in_specs=[smem, smem, smem, vmem] + [anyw...  9.48 us
    pallas_call x1, Pallas kernels, prepare(): pl.pallas_call(prepare_kernel, grid=(ROWS // ROW_BLOCK + 1,), in_specs=[p...  8.81 us
    pallas_call x1, Pallas kernels, forward(): pl.pallas_call(forward_kernel, in_specs=[pl.BlockSpec(memory_space=pl.ANY...  5.43 us
    pallas_call x1, Pallas kernels, inverse(): pl.pallas_call(inverse_kernel, in_specs=[pl.BlockSpec(memory_space=pl.ANY...  3.32 us
  transfers between devices with their start and end apart: 1, of which 1 were waited for; matrix products, arithmetic and copies ran while one was open for 0% of the time, Pallas kernels for 11%

profile of v3, /device:TPU:1, one launch (start us, length us, event | category | flops | bytes accessed | tf_op | source)
XLA Modules:
  0.0 82.9 jit_solution(2349020586564578326)
XLA Ops:
  0.6 5.4 %forward.1 = (f32[1024,128]{1,0:T(8,128)}, bf16[2,2,2,256,1024]{4,3,2,1,0:T(8,128)(2,1)}) custom-call(s32[2,128]{1,0:T(2,128)} %bitcast.16, f32[128,4096]{1,0:T(8,128)} %bitcast.21), custom_call_target="tpu_custom_call" | custom-call | tf_op jit(solution)/shard_map/forward/pallas_call | solution.py:165
  6.1 15.7 %all-to-all-start = ((f32[256,4,128]{2,1,0:T(4,128)}), f32[256,4,128]{2,1,0:T(4,128)S(1)}, u32[]{:S(2)}, u32[]{:S(2)}) async-start(f32[256,4,128]{2,1,0:T(4,128)} %bitcast.23), calls=%async_computation | async-start | bytes 1048576 | tf_op jit(solution)/shard_map/all_to_all | solution.py:496
  21.7 0.0 copy-start.1
  21.7 0.0 copy-start.2
  21.8 0.0 copy-start.3
  21.8 0.0 copy-start.4
  21.8 0.0 copy-start.5
  21.8 8.8 %prepare.1 = (bf16[2176,1024]{1,0:T(8,128)(2,1)}, bf16[2176,1024]{1,0:T(8,128)(2,1)}) custom-call(f32[16392,128]{1,0:T(8,128)} %bitcast.20), custom_call_target="tpu_custom_call" | custom-call | flops 20000000 | bytes 18000000 | tf_op jit(solution)/shard_map/prepare/pallas_call | solution.py:229
  30.6 12.4 %all-to-all-done = f32[256,4,128]{2,1,0:T(4,128)S(1)} async-done(((f32[256,4,128]{2,1,0:T(4,128)}), f32[256,4,128]{2,1,0:T(4,128)S(1)}, u32[]{:S(2)}, u32[]{:S(2)}) %all-to-all-start) | async-done | bytes 524320 | tf_op jit(solution)/shard_map/all_to_all | solution.py:496
  43.0 0.0 copy-done.1
  43.0 0.0 copy-done.2
  43.0 0.0 copy-done.3
  43.0 0.0 copy-done.4
  43.0 0.0 copy-done.5
  43.0 0.0 copy-start
  43.0 9.5 %legendre.1 = (f32[32,2049]{1,0:T(8,128)}, f32[1024,128]{1,0:T(8,128)S(1)}) custom-call(s32[256]{0:T(256)S(1)} %copy-done.2, s32[2,16]{1,0:T(2,128)S(1)} %bitcast.19, f32[16]{0:T(128)S(1)} %copy-done.5, f32[1024,128]{1,0:T(8,128)S(1)} %bitcast.12, bf16[2176,1024]{1,0:T(8,128)(2,1)} %get-tuple-element.9.high_hbm, ...), custom_call_target="tpu_custom_call" | custom-call | tf_op jit(solution)/shard_map/legendre/pallas_call | solution.py:391
  52.5 27.0 %all_to_all.10 = f32[256,4,128]{2,1,0:T(4,128)S(1)} all-to-all(f32[256,4,128]{2,1,0:T(4,128)S(1)} %bitcast.14), channel_id=1, replica_groups=mesh['lat'=64,'lev'=4] {'lat','lev'}, dimensions={0} | all-to-all | bytes 1048576 | tf_op jit(solution)/shard_map/all_to_all | solution.py:496
  79.5 0.0 copy-done
  79.5 3.3 %inverse.1 = f32[128,4096]{1,0:T(8,128)} custom-call(s32[2,128]{1,0:T(2,128)S(1)} %bitcast.17, f32[1024,128]{1,0:T(8,128)S(1)} %bitcast.13, bf16[2,2,2,256,1024]{4,3,2,1,0:T(8,128)(2,1)S(1)} %copy-done), custom_call_target="tpu_custom_call" | custom-call | tf_op jit(solution)/shard_map/inverse/pallas_call | solution.py:478
Async XLA Ops:
  6.1 36.9 %all-to-all-start = ((f32[256,4,128]{2,1,0:T(4,128)}), f32[256,4,128]{2,1,0:T(4,128)S(1)}, u32[]{:S(2)}, u32[]{:S(2)}) async-start(f32[256,4,128]{2,1,0:T(4,128)} %bitcast.23), calls=%async_computation | async-start | bytes 1048576 | tf_op jit(solution)/shard_map/all_to_all | solution.py:496
  21.7 21.2 %copy-start.1 = (f32[1,2,16,2049]{3,2,1,0:T(8,128)S(1)}, f32[1,2,16,2049]{3,2,1,0:T(8,128)}, u32[]{:S(2)}) copy-start(f32[1,2,16,2049]{3,2,1,0:T(8,128)} %param.8) | copy-start | bytes 786820
  21.7 21.2 %copy-start.2 = (s32[256]{0:T(256)S(1)}, s32[256]{0:T(256)}, u32[]{:S(2)}) copy-start(s32[256]{0:T(256)} %waves_ref.1) | copy-start | bytes 3076
  21.8 21.2 %copy-start.3 = (f32[1024]{0:T(1024)S(1)}, f32[1024]{0:T(1024)}, u32[]{:S(2)}) copy-start(f32[1024]{0:T(1024)} %param.10) | copy-start | bytes 12292
  21.8 21.2 %copy-start.4 = (s32[16,2]{0,1:T(2,128)S(1)}, s32[16,2]{0,1:T(2,128)}, u32[]{:S(2)}) copy-start(s32[16,2]{0,1:T(2,128)} %param.13) | copy-start | bytes 388
  21.8 21.2 %copy-start.5 = (f32[16]{0:T(128)S(1)}, f32[16]{0:T(128)}, u32[]{:S(2)}) copy-start(f32[16]{0:T(128)} %diffusion_ref.1) | copy-start | bytes 196
  43.0 36.5 %copy-start = (bf16[2,2,2,256,1024]{4,3,2,1,0:T(8,128)(2,1)S(1)}, bf16[2,2,2,256,1024]{4,3,2,1,0:T(8,128)(2,1)}, u32[]{:S(2)}) copy-start(bf16[2,2,2,256,1024]{4,3,2,1,0:T(8,128)(2,1)} %get-tuple-element.12.table) | copy-start | bytes 12582916

commit v4 on v3

--- a/solution.py
+++ b/solution.py
@@ -19,7 +19,7 @@
 LEV = 16
 ROW_BLOCK = 512
 ROWS_PAD = 2176
-CHUNKS = (0, 1024, ROWS_PAD)
+CHUNKS = (0, 896, ROWS_PAD)
 LON_CUTS = (0, 512, 768, 1024)
 VMEM = 58 * 1024 * 1024
 VMEM_LEGENDRE = 52 * 1024 * 1024

time: 83.1 us -> 83 us (level)
  no operation moved by 1% of the time
where the time goes in v4:
time: 83 us; the launch traced here: 82.8 us
  blocking collectives  27 us (33%)
  Pallas kernels  26.9 us (32%)
  starting transfers between devices  15.7 us (19%)
  waiting for transfers between devices  12.4 us (15%)
  between operations  0.88 us (1%)
    all_to_all x1, blocking collectives, exchange(): lax.all_to_all(block.reshape(PAIRS, 4, 128), ('lat', 'lev'), 0, 0, tiled=...  27 us
    all_to_all x1, starting transfers between devices, exchange(): lax.all_to_all(block.reshape(PAIRS, 4, 128), ('lat', 'lev'), 0, 0, tiled=...  15.7 us
    all_to_all x1, waiting for transfers between devices, exchange(): lax.all_to_all(block.reshape(PAIRS, 4, 128), ('lat', 'lev'), 0, 0, tiled=...  12.4 us
    pallas_call x1, Pallas kernels, legendre(): pl.pallas_call(legendre_kernel, in_specs=[smem, smem, smem, vmem] + [anyw...  9.31 us
    pallas_call x1, Pallas kernels, prepare(): pl.pallas_call(prepare_kernel, grid=(ROWS // ROW_BLOCK + 1,), in_specs=[p...  8.81 us
    pallas_call x1, Pallas kernels, forward(): pl.pallas_call(forward_kernel, in_specs=[pl.BlockSpec(memory_space=pl.ANY...  5.43 us
    pallas_call x1, Pallas kernels, inverse(): pl.pallas_call(inverse_kernel, in_specs=[pl.BlockSpec(memory_space=pl.ANY...  3.32 us
  transfers between devices with their start and end apart: 1, of which 1 were waited for; matrix products, arithmetic and copies ran while one was open for 0% of the time, Pallas kernels for 11%

profile of v4, /device:TPU:1, one launch (start us, length us, event | category | flops | bytes accessed | tf_op | source)
XLA Modules:
  0.0 82.8 jit_solution(329770730711032114)
XLA Ops:
  0.6 5.4 %forward.1 = (f32[1024,128]{1,0:T(8,128)}, bf16[2,2,2,256,1024]{4,3,2,1,0:T(8,128)(2,1)}) custom-call(s32[2,128]{1,0:T(2,128)} %bitcast.16, f32[128,4096]{1,0:T(8,128)} %bitcast.21), custom_call_target="tpu_custom_call" | custom-call | tf_op jit(solution)/shard_map/forward/pallas_call | solution.py:165
  6.1 15.7 %all-to-all-start = ((f32[256,4,128]{2,1,0:T(4,128)}), f32[256,4,128]{2,1,0:T(4,128)S(1)}, u32[]{:S(2)}, u32[]{:S(2)}) async-start(f32[256,4,128]{2,1,0:T(4,128)} %bitcast.23), calls=%async_computation | async-start | bytes 1048576 | tf_op jit(solution)/shard_map/all_to_all | solution.py:496
  21.7 0.0 copy-start.1
  21.7 0.0 copy-start.2
  21.8 0.0 copy-start.3
  21.8 0.0 copy-start.4
  21.8 0.0 copy-start.5
  21.8 8.8 %prepare.1 = (bf16[2176,1024]{1,0:T(8,128)(2,1)}, bf16[2176,1024]{1,0:T(8,128)(2,1)}) custom-call(f32[16392,128]{1,0:T(8,128)} %bitcast.20), custom_call_target="tpu_custom_call" | custom-call | flops 20000000 | bytes 18000000 | tf_op jit(solution)/shard_map/prepare/pallas_call | solution.py:229
  30.6 12.4 %all-to-all-done = f32[256,4,128]{2,1,0:T(4,128)S(1)} async-done(((f32[256,4,128]{2,1,0:T(4,128)}), f32[256,4,128]{2,1,0:T(4,128)S(1)}, u32[]{:S(2)}, u32[]{:S(2)}) %all-to-all-start) | async-done | bytes 524320 | tf_op jit(solution)/shard_map/all_to_all | solution.py:496
  43.0 0.0 copy-done.1
  43.0 0.0 copy-done.2
  43.0 0.0 copy-done.3
  43.0 0.0 copy-done.4
  43.0 0.0 copy-done.5
  43.0 0.0 copy-start
  43.0 9.3 %legendre.1 = (f32[32,2049]{1,0:T(8,128)}, f32[1024,128]{1,0:T(8,128)S(1)}) custom-call(s32[256]{0:T(256)S(1)} %copy-done.2, s32[2,16]{1,0:T(2,128)S(1)} %bitcast.19, f32[16]{0:T(128)S(1)} %copy-done.5, f32[1024,128]{1,0:T(8,128)S(1)} %bitcast.12, bf16[2176,1024]{1,0:T(8,128)(2,1)} %get-tuple-element.9.high_hbm, ...), custom_call_target="tpu_custom_call" | custom-call | tf_op jit(solution)/shard_map/legendre/pallas_call | solution.py:391
  52.3 27.0 %all_to_all.10 = f32[256,4,128]{2,1,0:T(4,128)S(1)} all-to-all(f32[256,4,128]{2,1,0:T(4,128)S(1)} %bitcast.14), channel_id=1, replica_groups=mesh['lat'=64,'lev'=4] {'lat','lev'}, dimensions={0} | all-to-all | bytes 1048576 | tf_op jit(solution)/shard_map/all_to_all | solution.py:496
  79.3 0.0 copy-done
  79.3 3.3 %inverse.1 = f32[128,4096]{1,0:T(8,128)} custom-call(s32[2,128]{1,0:T(2,128)S(1)} %bitcast.17, f32[1024,128]{1,0:T(8,128)S(1)} %bitcast.13, bf16[2,2,2,256,1024]{4,3,2,1,0:T(8,128)(2,1)S(1)} %copy-done), custom_call_target="tpu_custom_call" | custom-call | tf_op jit(solution)/shard_map/inverse/pallas_call | solution.py:478
Async XLA Ops:
  6.1 36.9 %all-to-all-start = ((f32[256,4,128]{2,1,0:T(4,128)}), f32[256,4,128]{2,1,0:T(4,128)S(1)}, u32[]{:S(2)}, u32[]{:S(2)}) async-start(f32[256,4,128]{2,1,0:T(4,128)} %bitcast.23), calls=%async_computation | async-start | bytes 1048576 | tf_op jit(solution)/shard_map/all_to_all | solution.py:496
  21.7 21.2 %copy-start.1 = (f32[1,2,16,2049]{3,2,1,0:T(8,128)S(1)}, f32[1,2,16,2049]{3,2,1,0:T(8,128)}, u32[]{:S(2)}) copy-start(f32[1,2,16,2049]{3,2,1,0:T(8,128)} %param.8) | copy-start | bytes 786820
  21.7 21.2 %copy-start.2 = (s32[256]{0:T(256)S(1)}, s32[256]{0:T(256)}, u32[]{:S(2)}) copy-start(s32[256]{0:T(256)} %waves_ref.1) | copy-start | bytes 3076
  21.8 21.2 %copy-start.3 = (f32[1024]{0:T(1024)S(1)}, f32[1024]{0:T(1024)}, u32[]{:S(2)}) copy-start(f32[1024]{0:T(1024)} %param.10) | copy-start | bytes 12292
  21.8 21.2 %copy-start.4 = (s32[16,2]{0,1:T(2,128)S(1)}, s32[16,2]{0,1:T(2,128)}, u32[]{:S(2)}) copy-start(s32[16,2]{0,1:T(2,128)} %param.13) | copy-start | bytes 388
  21.8 21.2 %copy-start.5 = (f32[16]{0:T(128)S(1)}, f32[16]{0:T(128)}, u32[]{:S(2)}) copy-start(f32[16]{0:T(128)} %diffusion_ref.1) | copy-start | bytes 196
  43.0 36.3 %copy-start = (bf16[2,2,2,256,1024]{4,3,2,1,0:T(8,128)(2,1)S(1)}, bf16[2,2,2,256,1024]{4,3,2,1,0:T(8,128)(2,1)}, u32[]{:S(2)}) copy-start(bf16[2,2,2,256,1024]{4,3,2,1,0:T(8,128)(2,1)} %get-tuple-element.12.table) | copy-start | bytes 12582916

commit v5 on v3

--- a/solution.py
+++ b/solution.py
@@ -416,7 +416,7 @@
 
 
 def inverse_kernel(
-    waves_hbm, received_ref, table, out_hbm, waves_ref, turned, grid, load_sems, store_sems
+    waves_ref, received_ref, table, out_hbm, turned, grid, store_sems
 ):
     count = len(LON_CUTS) - 1
 
@@ -430,10 +430,7 @@
         cols = pl.ds(cols.start, cols.stop - cols.start)
         return pltpu.make_async_copy(grid.at[:, cols], out_hbm.at[:, cols], store_sems.at[index, part])
 
-    load_waves = pltpu.make_async_copy(waves_hbm, waves_ref, load_sems.at[2])
-    load_waves.start()
     parts = regroup([received_ref[pl.ds(level, PAIRS, stride=4), :] for level in range(4)])
-    load_waves.wait()
     waves = wave_columns(waves_ref)
     for parity in range(2):
         half_cos, half_sin = cos_sin(waves[parity])
@@ -477,14 +474,12 @@
     vmem = pl.BlockSpec(memory_space=pltpu.VMEM)
     return pl.pallas_call(
         inverse_kernel,
-        in_specs=[pl.BlockSpec(memory_space=pl.ANY), vmem, vmem],
+        in_specs=[vmem, vmem, vmem],
         out_specs=pl.BlockSpec(memory_space=pl.ANY),
         out_shape=jax.ShapeDtypeStruct((128, NLON), jnp.float32),
         scratch_shapes=[
-            pltpu.VMEM((PAIRS // 128, 128), jnp.int32),
             pltpu.VMEM((2, 2, 256, 2 * PAIRS), jnp.bfloat16),
             pltpu.VMEM((128, NLON), jnp.float32),
-            pltpu.SemaphoreType.DMA((3,)),
             pltpu.SemaphoreType.DMA((len(LON_CUTS) - 1, 4)),
         ],
         compiler_params=pltpu.CompilerParams(vmem_limit_bytes=VMEM_INVERSE),

time: 83.1 us -> 82.8 us (level)
  no operation moved by 1% of the time
where the time goes in v5:
time: 82.8 us; the launch traced here: 82.6 us
  blocking collectives  27 us (33%)
  Pallas kernels  26.7 us (32%)
  starting transfers between devices  15.7 us (19%)
  waiting for transfers between devices  12.4 us (15%)
  between operations  0.88 us (1%)
    all_to_all x1, blocking collectives, exchange(): lax.all_to_all(block.reshape(PAIRS, 4, 128), ('lat', 'lev'), 0, 0, tiled=...  27 us
    all_to_all x1, starting transfers between devices, exchange(): lax.all_to_all(block.reshape(PAIRS, 4, 128), ('lat', 'lev'), 0, 0, tiled=...  15.7 us
    all_to_all x1, waiting for transfers between devices, exchange(): lax.all_to_all(block.reshape(PAIRS, 4, 128), ('lat', 'lev'), 0, 0, tiled=...  12.4 us
    pallas_call x1, Pallas kernels, legendre(): pl.pallas_call(legendre_kernel, in_specs=[smem, smem, smem, vmem] + [anyw...  9.48 us
    pallas_call x1, Pallas kernels, prepare(): pl.pallas_call(prepare_kernel, grid=(ROWS // ROW_BLOCK + 1,), in_specs=[p...  8.81 us
    pallas_call x1, Pallas kernels, forward(): pl.pallas_call(forward_kernel, in_specs=[pl.BlockSpec(memory_space=pl.ANY...  5.43 us
    pallas_call x1, Pallas kernels, inverse(): pl.pallas_call(inverse_kernel, in_specs=[vmem, vmem, vmem], out_specs=pl....  2.99 us
  transfers between devices with their start and end apart: 1, of which 1 were waited for; matrix products, arithmetic and copies ran while one was open for 0% of the time, Pallas kernels for 11%

profile of v5, /device:TPU:1, one launch (start us, length us, event | category | flops | bytes accessed | tf_op | source)
XLA Modules:
  0.0 82.6 jit_solution(6731569920359700172)
XLA Ops:
  0.6 5.4 %forward.1 = (f32[1024,128]{1,0:T(8,128)}, bf16[2,2,2,256,1024]{4,3,2,1,0:T(8,128)(2,1)}) custom-call(s32[2,128]{1,0:T(2,128)} %bitcast.16, f32[128,4096]{1,0:T(8,128)} %bitcast.21), custom_call_target="tpu_custom_call" | custom-call | tf_op jit(solution)/shard_map/forward/pallas_call | solution.py:165
  6.1 15.7 %all-to-all-start = ((f32[256,4,128]{2,1,0:T(4,128)}), f32[256,4,128]{2,1,0:T(4,128)S(1)}, u32[]{:S(2)}, u32[]{:S(2)}) async-start(f32[256,4,128]{2,1,0:T(4,128)} %bitcast.23), calls=%async_computation | async-start | bytes 1048576 | tf_op jit(solution)/shard_map/all_to_all | solution.py:491
  21.7 0.0 copy-start.1
  21.7 0.0 copy-start.2
  21.8 0.0 copy-start.3
  21.8 0.0 copy-start.4
  21.8 0.0 copy-start.5
  21.8 8.8 %prepare.1 = (bf16[2176,1024]{1,0:T(8,128)(2,1)}, bf16[2176,1024]{1,0:T(8,128)(2,1)}) custom-call(f32[16392,128]{1,0:T(8,128)} %bitcast.20), custom_call_target="tpu_custom_call" | custom-call | flops 20000000 | bytes 18000000 | tf_op jit(solution)/shard_map/prepare/pallas_call | solution.py:229
  30.6 12.4 %all-to-all-done = f32[256,4,128]{2,1,0:T(4,128)S(1)} async-done(((f32[256,4,128]{2,1,0:T(4,128)}), f32[256,4,128]{2,1,0:T(4,128)S(1)}, u32[]{:S(2)}, u32[]{:S(2)}) %all-to-all-start) | async-done | bytes 524320 | tf_op jit(solution)/shard_map/all_to_all | solution.py:491
  43.0 0.0 copy-done.1
  43.0 0.0 copy-done.2
  43.0 0.0 copy-done.3
  43.0 0.0 copy-done.4
  43.0 0.0 copy-done.5
  43.0 0.0 copy-start
  43.0 9.5 %legendre.1 = (f32[32,2049]{1,0:T(8,128)}, f32[1024,128]{1,0:T(8,128)S(1)}) custom-call(s32[256]{0:T(256)S(1)} %copy-done.2, s32[2,16]{1,0:T(2,128)S(1)} %bitcast.19, f32[16]{0:T(128)S(1)} %copy-done.5, f32[1024,128]{1,0:T(8,128)S(1)} %bitcast.12, bf16[2176,1024]{1,0:T(8,128)(2,1)} %get-tuple-element.9.high_hbm, ...), custom_call_target="tpu_custom_call" | custom-call | tf_op jit(solution)/shard_map/legendre/pallas_call | solution.py:391
  52.5 27.0 %all_to_all.10 = f32[256,4,128]{2,1,0:T(4,128)S(1)} all-to-all(f32[256,4,128]{2,1,0:T(4,128)S(1)} %bitcast.14), channel_id=1, replica_groups=mesh['lat'=64,'lev'=4] {'lat','lev'}, dimensions={0} | all-to-all | bytes 1048576 | tf_op jit(solution)/shard_map/all_to_all | solution.py:491
  79.5 0.0 copy-done
  79.5 3.0 %inverse.1 = f32[128,4096]{1,0:T(8,128)} custom-call(s32[2,128]{1,0:T(2,128)S(1)} %bitcast.17, f32[1024,128]{1,0:T(8,128)S(1)} %bitcast.13, bf16[2,2,2,256,1024]{4,3,2,1,0:T(8,128)(2,1)S(1)} %copy-done), custom_call_target="tpu_custom_call" | custom-call | tf_op jit(solution)/shard_map/inverse/pallas_call | solution.py:475
Async XLA Ops:
  6.1 36.9 %all-to-all-start = ((f32[256,4,128]{2,1,0:T(4,128)}), f32[256,4,128]{2,1,0:T(4,128)S(1)}, u32[]{:S(2)}, u32[]{:S(2)}) async-start(f32[256,4,128]{2,1,0:T(4,128)} %bitcast.23), calls=%async_computation | async-start | bytes 1048576 | tf_op jit(solution)/shard_map/all_to_all | solution.py:491
  21.7 21.2 %copy-start.1 = (f32[1,2,16,2049]{3,2,1,0:T(8,128)S(1)}, f32[1,2,16,2049]{3,2,1,0:T(8,128)}, u32[]{:S(2)}) copy-start(f32[1,2,16,2049]{3,2,1,0:T(8,128)} %param.8) | copy-start | bytes 786820
  21.7 21.2 %copy-start.2 = (s32[256]{0:T(256)S(1)}, s32[256]{0:T(256)}, u32[]{:S(2)}) copy-start(s32[256]{0:T(256)} %waves_ref.1) | copy-start | bytes 3076
  21.8 21.2 %copy-start.3 = (f32[1024]{0:T(1024)S(1)}, f32[1024]{0:T(1024)}, u32[]{:S(2)}) copy-start(f32[1024]{0:T(1024)} %param.10) | copy-start | bytes 12292
  21.8 21.2 %copy-start.4 = (s32[16,2]{0,1:T(2,128)S(1)}, s32[16,2]{0,1:T(2,128)}, u32[]{:S(2)}) copy-start(s32[16,2]{0,1:T(2,128)} %param.13) | copy-start | bytes 388
  21.8 21.2 %copy-start.5 = (f32[16]{0:T(128)S(1)}, f32[16]{0:T(128)}, u32[]{:S(2)}) copy-start(f32[16]{0:T(128)} %diffusion_ref.1) | copy-start | bytes 196
  43.0 36.5 %copy-start = (bf16[2,2,2,256,1024]{4,3,2,1,0:T(8,128)(2,1)S(1)}, bf16[2,2,2,256,1024]{4,3,2,1,0:T(8,128)(2,1)}, u32[]{:S(2)}) copy-start(bf16[2,2,2,256,1024]{4,3,2,1,0:T(8,128)(2,1)} %get-tuple-element.12.table) | copy-start | bytes 12582916
